TPU v7x, 32 devices: a whole 2x2x4 slice. The times are simulated.
32 devices in a mesh: leaf: 4 (over z), sub: 8 (over y, x, core).
Axes of the slice: x: 2, y: 2, z: 4, core: 2. Of those that a mesh axis runs over, the one named last changes fastest.
Arguments:
- right_side: float32 [65536, 256], P(('leaf', 'sub')), may hold values from -6 to 6
- u_bases: float32 [4, 65536, 256], P(None, ('leaf', 'sub')), may hold values from -6 to 6
- v_bases: float32 [4, 65536, 256], P(None, ('leaf', 'sub')), may hold values from -0.00271875 to 0.00271875
Outputs:
- solution: float32 [65536, 256], P(('leaf', 'sub'))
All inputs are finite; a program needn't handle non-finite values.
Results may differ from a plain program's by a relative error of at most 0.00022.
Values sent between devices are 32-bit elements; how exact they have to be, the bound alone decides.
A program may use at most 128 MiB of HBM per device.

v0:
```python
import functools

import jax
import jax.numpy as jnp
from jax import lax
from jax.experimental import pallas as pl
from jax.experimental.pallas import tpu as pltpu
from jax.sharding import PartitionSpec as P

AXES = ("leaf", "sub")
F32 = jnp.float32
VMEM_LIMIT = 56 * 1024 * 1024
SETTLED = 4e-6
MOST_SWEEPS = 12


def split(x):
    high = x.astype(jnp.bfloat16)
    return high, (x - high.astype(F32)).astype(jnp.bfloat16)


def dot(a, b):
    return jnp.dot(a, b, preferred_element_type=F32)


def mm(a, b):
    a_high, a_low = split(a)
    b_high, b_low = split(b)
    return dot(a_high, b_high) + (dot(a_high, b_low) + dot(a_low, b_high))


def joined(parity, mine, other):
    first = jnp.where(parity == 0, mine, other)
    second = jnp.where(parity == 0, other, mine)
    return jnp.concatenate([first, second], axis=1)


def gram_kernel(par_ref, v_ref, b_ref, u_ref, mine_ref, other_ref, acc):
    step = pl.program_id(0)
    levels, _, rank = v_ref.shape
    half = rank // 2

    @pl.when(step == 0)
    def _():
        acc[...] = jnp.zeros_like(acc)

    stacked = []
    for j in range(u_ref.shape[0] + 1):
        high, low = split(b_ref[...] if j == 0 else u_ref[j - 1])
        stacked.append(jnp.concatenate([high, low, high], axis=0))
    for k in range(levels):
        high, low = split(v_ref[k])
        rows = jnp.concatenate([high, high, low], axis=0).T
        for j, block in enumerate(stacked):
            product = dot(rows, block)
            place = (pl.ds(k * rank, rank), pl.ds(j * half, half))
            acc[(0,) + place] += product[:, :half]
            acc[(1,) + place] += product[:, half:]

    @pl.when(step == pl.num_programs(0) - 1)
    def _():
        mine_ref[...] = acc[par_ref[0]]
        other_ref[...] = acc[1 - par_ref[0]]


def gram(parity, v, b, u, first, levels, tile):
    level_count, rows, rank = u.shape
    width = (level_count + 1) * rank // 2
    shape = jax.ShapeDtypeStruct((levels * rank, width), F32)
    whole = pl.BlockSpec((levels * rank, width), lambda i: (0, 0))
    return pl.pallas_call(
        gram_kernel,
        grid=(rows // tile,),
        out_shape=(shape, shape),
        in_specs=[
            pl.BlockSpec(memory_space=pltpu.SMEM),
            pl.BlockSpec((levels, tile, rank), lambda i: (first // levels, i, 0)),
            pl.BlockSpec((tile, rank), lambda i: (i, 0)),
            pl.BlockSpec((level_count, tile, rank), lambda i: (0, i, 0)),
        ],
        out_specs=(whole, whole),
        scratch_shapes=[pltpu.VMEM((2, levels * rank, width), F32)],
        compiler_params=pltpu.CompilerParams(vmem_limit_bytes=VMEM_LIMIT),
        cost_estimate=pl.CostEstimate(
            flops=12 * levels * rank * width * rows,
            bytes_accessed=4 * rows * rank * (levels + level_count + 1) + 8 * levels * rank * width,
            transcendentals=0,
        ),
    )(parity, v, b, u)


def solve_values(parity, own_ref, sib_ref, own_other_ref, sib_other_ref):
    half = own_other_ref.shape[1]
    width = own_ref.shape[1] - half
    own_rank = joined(parity, own_ref[:, width:], own_other_ref[...])
    sib_rank = joined(parity, sib_ref[:, width:], sib_other_ref[...])
    terms = sib_ref[:, :width] - mm(sib_rank, own_ref[:, :width])
    power = mm(sib_rank, own_rank)
    answer = terms + mm(power, terms)

    def going(state):
        count, size, _, _ = state
        return jnp.logical_and(size > SETTLED, count < MOST_SWEEPS)

    def sweep(state):
        count, _, power, answer = state
        power = mm(power, power)
        answer = answer + mm(power, answer)
        return count + 1, jnp.sum(power * power), power, answer

    state = (jnp.int32(1), jnp.sum(power * power), power, answer)
    return lax.while_loop(going, sweep, state)[3]


def solve_kernel(par_ref, own_ref, sib_ref, own_other_ref, sib_other_ref, row_ref, col_ref, col_other_ref, z_ref, next_ref):
    parity = par_ref[0]
    answer = solve_values(parity, own_ref, sib_ref, own_other_ref, sib_other_ref)
    z_ref[...] = answer
    column = joined(parity, col_ref[...], col_other_ref[...])
    next_ref[...] = row_ref[...] - mm(column, answer)


def top_kernel(count, par_ref, own_ref, sib_ref, own_other_ref, sib_other_ref, *refs):
    parity = par_ref[0]
    z_refs, z_other_refs, out_ref = refs[:count], refs[count : 2 * count], refs[-1]
    rank = own_ref.shape[0]
    half = own_other_ref.shape[1]
    weights = [solve_values(parity, own_ref, sib_ref, own_other_ref, sib_other_ref)]
    for k in range(1, count + 1):
        weight = z_refs[k - 1][:, :half]
        for j in range(k):
            mine = z_refs[k - 1][:, (j + 1) * half : (j + 2) * half]
            other = z_other_refs[k - 1][:, j * half : (j + 1) * half]
            weight = weight - mm(joined(parity, mine, other), weights[j])
        weights.append(weight)
    for k, weight in enumerate(weights):
        out_ref[k * rank : (k + 1) * rank, :] = weight


def small_call(kernel, shapes, parity, *arrays):
    specs = [pl.BlockSpec(memory_space=pltpu.VMEM)]
    return pl.pallas_call(
        kernel,
        out_shape=shapes,
        in_specs=[pl.BlockSpec(memory_space=pltpu.SMEM)] + specs * len(arrays),
        out_specs=jax.tree.map(lambda _: specs[0], shapes),
        compiler_params=pltpu.CompilerParams(vmem_limit_bytes=VMEM_LIMIT),
        cost_estimate=pl.CostEstimate(flops=3 * 10**9, bytes_accessed=4 * 10**6, transcendentals=0),
    )(parity, *arrays)


def apply_kernel(par_ref, b_ref, u_ref, w_ref, w_other_ref, out_ref, high, low):
    levels, _, rank = u_ref.shape

    @pl.when(pl.program_id(0) == 0)
    def _():
        high[...], low[...] = split(joined(par_ref[0], w_ref[...], w_other_ref[...]))

    total = b_ref[...]
    for k in range(levels):
        u_high, u_low = split(u_ref[k])
        rows = pl.ds(k * rank, rank)
        total = total - (
            dot(u_high, high[rows, :]) + (dot(u_high, low[rows, :]) + dot(u_low, high[rows, :]))
        )
    out_ref[...] = total


def apply(parity, b, u, w, w_other, tile):
    levels, rows, rank = u.shape
    width = b.shape[1]
    half = pl.BlockSpec(w.shape, lambda i: (0, 0))
    return pl.pallas_call(
        apply_kernel,
        grid=(rows // tile,),
        out_shape=jax.ShapeDtypeStruct(b.shape, F32),
        in_specs=[
            pl.BlockSpec(memory_space=pltpu.SMEM),
            pl.BlockSpec((tile, width), lambda i: (i, 0)),
            pl.BlockSpec((levels, tile, rank), lambda i: (0, i, 0)),
            half,
            half,
        ],
        out_specs=pl.BlockSpec((tile, width), lambda i: (i, 0)),
        scratch_shapes=[pltpu.VMEM((levels * rank, width), jnp.bfloat16)] * 2,
        compiler_params=pltpu.CompilerParams(vmem_limit_bytes=VMEM_LIMIT),
    )(parity, b, u, w, w_other)


def swap(block, even_bit, odd_bit):
    count = lax.axis_size(AXES)
    route = [(i, i ^ (1 << (odd_bit if i & 1 else even_bit))) for i in range(count)]
    return lax.ppermute(block, AXES, route)


def local(b, u, v):
    depth = lax.axis_size(AXES).bit_length() - 1
    levels, row_count, rank = u.shape
    half = rank // 2
    tile = min(512, row_count)
    parity = (lax.axis_index(AXES) & 1).reshape(1)

    top, top_other = gram(parity, v, b, u, levels - 1, 1, tile)
    low, low_other = gram(parity, v, b, u, 0, levels - 1, tile)
    top = top + swap(top_other, 0, 0)
    low = low + swap(low_other, 0, 0)
    rows = [low[k * rank : (k + 1) * rank] for k in range(levels - 1)] + [top]

    answers, answers_other = [None] * levels, [None] * levels
    for k in range(levels - 1, -1, -1):
        width = (k + 1) * half
        sibling = depth - 1 - k
        own = rows[k][:, : width + half]
        for step in range(1, sibling):
            own = own + swap(own, step, step % (sibling - 1) + 1)
        sib = swap(own, sibling, sibling)
        own_other = swap(own[:, width:], 0, 0)
        sib_other = swap(sib[:, width:], 0, 0)
        if k > 0:
            cols = jnp.concatenate([rows[i][:, width : width + half] for i in range(k)], axis=0)
            cols_other = swap(cols, 0, 0)
            last = slice((k - 1) * rank, k * rank)
            shape = jax.ShapeDtypeStruct((rank, width), F32)
            z, following = small_call(
                solve_kernel, (shape, shape), parity, own, sib, own_other, sib_other,
                rows[k - 1][:, :width], cols[last], cols_other[last],
            )
            answers[k] = z
            answers_other[k] = swap(z[:, half:], 0, 0)
            rows[k - 1] = following
            if k > 1:
                before = slice(0, (k - 1) * rank)
                column = joined(parity[0], cols[before], cols_other[before])
                change = jnp.dot(column, z, precision=lax.Precision.HIGH, preferred_element_type=F32)
                for i in range(k - 1):
                    rows[i] = rows[i][:, :width] - change[i * rank : (i + 1) * rank]
        else:
            shape = jax.ShapeDtypeStruct((levels * rank, half), F32)
            weights = small_call(
                functools.partial(top_kernel, levels - 1), shape, parity, own, sib, own_other, sib_other,
                *answers[1:], *answers_other[1:],
            )
    return apply(parity, b, u, weights, swap(weights, 0, 0), tile)


def solution(mesh):
    return jax.shard_map(
        local,
        mesh=mesh,
        in_specs=(P(AXES, None), P(None, AXES, None), P(None, AXES, None)),
        out_specs=P(AXES, None),
        check_vma=False,
    )
```

profile of v0, /device:TPU:0, one launch (start us, length us, event | category | flops | bytes accessed | tf_op | source)
XLA Modules:
  0.0 181.9 jit_solution(10845381862939844477)
XLA Ops:
  0.0 17.9 %shard_map.38 = (f32[768,640]{1,0:T(8,128)}, f32[768,640]{1,0:T(8,128)}) custom-call(s32[1]{0:T(128)} %bitcast.par_ref, f32[4,2048,256]{2,1,0:T(8,128)} %v_ref.3, f32[2048,256]{1,0:T(8,128)} %b_ref.5, f32[4,2048,256]{2,1,0:T(8,128)} %u_ref.5), custom_call_target="tpu_custom_call" | custom-call | flops 12079595520 | bytes 20709376 | tf_op jit(solution)/shard_map/pallas_call | solution.py:71
  18.3 9.0 %shard_map.37 = (f32[256,640]{1,0:T(8,128)}, f32[256,640]{1,0:T(8,128)}) custom-call(s32[1]{0:T(128)} %bitcast.par_ref, f32[4,2048,256]{2,1,0:T(8,128)} %v_ref.3, f32[2048,256]{1,0:T(8,128)} %b_ref.5, f32[4,2048,256]{2,1,0:T(8,128)} %u_ref.5), custom_call_target="tpu_custom_call" | custom-call | flops 4026531840 | bytes 13893632 | tf_op jit(solution)/shard_map/pallas_call | solution.py:71
  27.4 2.2 %collective-permute-done = f32[256,640]{1,0:T(8,128)S(1)} collective-permute-done((f32[256,640]{1,0:T(8,128)}, f32[256,640]{1,0:T(8,128)S(1)}, u32[]{:S(2)}, u32[]{:S(2)}) %collective-permute-start) | collective-permute-done | bytes 655392 | tf_op jit(solution)/shard_map/ppermute | solution.py:193
  30.8 2.7 %collective-permute-start.1 = (f32[256,640]{1,0:T(8,128)S(1)}, f32[256,640]{1,0:T(8,128)S(1)}, u32[]{:S(2)}, u32[]{:S(2)}) collective-permute-start(f32[256,640]{1,0:T(8,128)S(1)} %add.28.own_ref), channel_id=1, source_target_pairs={{0,2},{1,3},{2,0},{3,1},{4,6},{5,7},{6,4},{7,5},{8,10},{9,11},{10,... | collective-permute-start | bytes 1966088 | tf_op jit(solution)/shard_map/ppermute | solution.py:193
  34.5 14.4 %collective-permute-done.1.sib_ref = f32[256,640]{1,0:T(8,128)S(1)} collective-permute-done((f32[256,640]{1,0:T(8,128)S(1)}, f32[256,640]{1,0:T(8,128)S(1)}, u32[]{:S(2)}, u32[]{:S(2)}) %collective-permute-start.1) | collective-permute-done | bytes 655392 | tf_op jit(solution)/shard_map/ppermute | solution.py:193
  52.5 5.7 %shard_map.39 = (f32[256,512]{1,0:T(8,128)}, f32[256,512]{1,0:T(8,128)}) custom-call(s32[1]{0:T(128)} %bitcast.par_ref, f32[256,640]{1,0:T(8,128)} %copy-done.3, f32[256,640]{1,0:T(8,128)} %copy-done.15, f32[256,128]{1,0:T(8,128)} %copy-done.23, f32[256,128]{1,0:T(8,128)} %copy-done.26, f32[256,512]{1,0:T(8,128)} %slice.130.row_ref, ...), custom_call_target="tpu_custom_call" | custom-call | flops 3000000000 | bytes 4000000 | tf_op jit(solution)/shard_map/pallas_call | solution.py:142
  61.6 11.1 %collective-permute-done.6 = f32[256,512]{1,0:T(8,128)S(1)} collective-permute-done((f32[256,512]{1,0:T(8,128)}, f32[256,512]{1,0:T(8,128)S(1)}, u32[]{:S(2)}, u32[]{:S(2)}) %collective-permute-start.6) | collective-permute-done | bytes 524320 | tf_op jit(solution)/shard_map/ppermute | solution.py:193
  72.8 2.6 %collective-permute-start.7 = (f32[256,512]{1,0:T(8,128)S(1)}, f32[256,512]{1,0:T(8,128)S(1)}, u32[]{:S(2)}, u32[]{:S(2)}) collective-permute-start(f32[256,512]{1,0:T(8,128)S(1)} %add.30.own_ref), channel_id=1, source_target_pairs={{0,4},{1,5},{2,6},{3,7},{4,0},{5,1},{6,2},{7,3},{8,12},{9,13},{10,... | collective-permute-start | bytes 1572872 | tf_op jit(solution)/shard_map/ppermute | solution.py:193
  77.2 10.1 %collective-permute-done.7.sib_ref = f32[256,512]{1,0:T(8,128)S(1)} collective-permute-done((f32[256,512]{1,0:T(8,128)S(1)}, f32[256,512]{1,0:T(8,128)S(1)}, u32[]{:S(2)}, u32[]{:S(2)}) %collective-permute-start.7) | collective-permute-done | bytes 524320 | tf_op jit(solution)/shard_map/ppermute | solution.py:193
  89.3 6.1 %shard_map.40 = (f32[256,384]{1,0:T(8,128)}, f32[256,384]{1,0:T(8,128)}) custom-call(s32[1]{0:T(128)} %bitcast.par_ref, f32[256,512]{1,0:T(8,128)} %copy-done.4, f32[256,512]{1,0:T(8,128)} %copy-done.14, f32[256,128]{1,0:T(8,128)} %copy-done.20, f32[256,128]{1,0:T(8,128)} %copy-done.25, f32[256,384]{1,0:T(8,128)} %slice.140.row_ref, f32[256,128]{1,0:T(8,128)} %copy-done.8, ...), custom_call_target="tpu_custom_call" | custom-call | flops 3000000000 | bytes 4000000 | tf_op jit(solution)/shard_map/pallas_call | solution.py:142
  96.8 6.5 %collective-permute-done.11 = f32[256,384]{1,0:T(8,128)S(1)} collective-permute-done((f32[256,384]{1,0:T(8,128)}, f32[256,384]{1,0:T(8,128)S(1)}, u32[]{:S(2)}, u32[]{:S(2)}) %collective-permute-start.11) | collective-permute-done | bytes 393248 | tf_op jit(solution)/shard_map/ppermute | solution.py:193
  104.4 1.8 collective-permute-start.12
  106.2 6.0 %collective-permute-done.12 = f32[256,384]{1,0:T(8,128)S(1)} collective-permute-done((f32[256,384]{1,0:T(8,128)S(1)}, f32[256,384]{1,0:T(8,128)S(1)}, u32[]{:S(2)}, u32[]{:S(2)}) %collective-permute-start.12) | collective-permute-done | bytes 393248 | tf_op jit(solution)/shard_map/ppermute | solution.py:193
  113.6 8.2 %collective-permute-done.13.sib_ref = f32[256,384]{1,0:T(8,128)S(1)} collective-permute-done((f32[256,384]{1,0:T(8,128)S(1)}, f32[256,384]{1,0:T(8,128)S(1)}, u32[]{:S(2)}, u32[]{:S(2)}) %collective-permute-start.13) | collective-permute-done | bytes 393248 | tf_op jit(solution)/shard_map/ppermute | solution.py:193
  124.0 5.1 %shard_map.41 = (f32[256,256]{1,0:T(8,128)}, f32[256,256]{1,0:T(8,128)}) custom-call(s32[1]{0:T(128)} %bitcast.par_ref, f32[256,384]{1,0:T(8,128)} %copy-done.5, f32[256,384]{1,0:T(8,128)} %copy-done.13, f32[256,128]{1,0:T(8,128)} %copy-done.24, f32[256,128]{1,0:T(8,128)} %copy-done.27, f32[256,256]{1,0:T(8,128)} %slice.150.row_ref, f32[256,128]{1,0:T(8,128)} %copy-done.10, ...), custom_call_target="tpu_custom_call" | custom-call | flops 3000000000 | bytes 4000000 | tf_op jit(solution)/shard_map/pallas_call | solution.py:142
  130.7 5.1 %collective-permute-done.17 = f32[256,256]{1,0:T(8,128)S(1)} collective-permute-done((f32[256,256]{1,0:T(8,128)}, f32[256,256]{1,0:T(8,128)S(1)}, u32[]{:S(2)}, u32[]{:S(2)}) %collective-permute-start.17) | collective-permute-done | bytes 262176 | tf_op jit(solution)/shard_map/ppermute | solution.py:193
  136.8 1.8 collective-permute-start.18
  138.6 4.6 %collective-permute-done.18 = f32[256,256]{1,0:T(8,128)S(1)} collective-permute-done((f32[256,256]{1,0:T(8,128)S(1)}, f32[256,256]{1,0:T(8,128)S(1)}, u32[]{:S(2)}, u32[]{:S(2)}) %collective-permute-start.18) | collective-permute-done | bytes 262176 | tf_op jit(solution)/shard_map/ppermute | solution.py:193
  143.7 6.0 %collective-permute-done.19 = f32[256,256]{1,0:T(8,128)S(1)} collective-permute-done((f32[256,256]{1,0:T(8,128)S(1)}, f32[256,256]{1,0:T(8,128)S(1)}, u32[]{:S(2)}, u32[]{:S(2)}) %collective-permute-start.19) | collective-permute-done | bytes 262176 | tf_op jit(solution)/shard_map/ppermute | solution.py:193
  149.7 2.8 %collective-permute-start.20 = (f32[256,256]{1,0:T(8,128)S(1)}, f32[256,256]{1,0:T(8,128)S(1)}, u32[]{:S(2)}, u32[]{:S(2)}) collective-permute-start(f32[256,256]{1,0:T(8,128)S(1)} %add.35.own_ref), channel_id=1, source_target_pairs={{0,16},{1,17},{2,18},{3,19},{4,20},{5,21},{6,22},{7,23},{8,24},{9,... | collective-permute-start | bytes 786440 | tf_op jit(solution)/shard_map/ppermute | solution.py:193
  153.3 9.2 %collective-permute-done.20.sib_ref = f32[256,256]{1,0:T(8,128)S(1)} collective-permute-done((f32[256,256]{1,0:T(8,128)S(1)}, f32[256,256]{1,0:T(8,128)S(1)}, u32[]{:S(2)}, u32[]{:S(2)}) %collective-permute-start.20) | collective-permute-done | bytes 262176 | tf_op jit(solution)/shard_map/ppermute | solution.py:193
  164.7 6.1 %shard_map.42.w_ref = f32[1024,128]{1,0:T(8,128)} custom-call(s32[1]{0:T(128)} %bitcast.par_ref, f32[256,256]{1,0:T(8,128)} %copy-done.6, f32[256,256]{1,0:T(8,128)} %copy-done.12, f32[256,128]{1,0:T(8,128)} %copy-done.19, f32[256,128]{1,0:T(8,128)} %copy-done.22, f32[256,256]{1,0:T(8,128)} %get-tuple-element.24.refs_0_, ...), custom_call_target="tpu_custom_call" | custom-call | flops 3000000000 | bytes 4000000 | tf_op jit(solution)/shard_map/pallas_call | solution.py:142
  170.9 2.0 %collective-permute-done.26.w_other_ref = f32[1024,128]{1,0:T(8,128)S(1)} collective-permute-done((f32[1024,128]{1,0:T(8,128)}, f32[1024,128]{1,0:T(8,128)S(1)}, u32[]{:S(2)}, u32[]{:S(2)}) %collective-permute-start.26) | collective-permute-done | bytes 524320 | tf_op jit(solution)/shard_map/ppermute | solution.py:193
  173.7 8.2 %shard_map.43 = f32[2048,256]{1,0:T(8,128)} custom-call(s32[1]{0:T(128)} %bitcast.par_ref, f32[2048,256]{1,0:T(8,128)} %b_ref.5, f32[4,2048,256]{2,1,0:T(8,128)} %u_ref.5, f32[1024,128]{1,0:T(8,128)} %shard_map.42.w_ref, f32[1024,128]{1,0:T(8,128)} %copy-done.9), custom_call_target="tpu_custom_call" | custom-call | tf_op jit(solution)/shard_map/pallas_call | solution.py:173
  (127 shorter events, 26.1 us)
Async XLA Ops:
  17.9 15.7 %collective-permute-start.4 = (f32[768,640]{1,0:T(8,128)}, f32[768,640]{1,0:T(8,128)S(1)}, u32[]{:S(2)}, u32[]{:S(2)}) collective-permute-start(f32[768,640]{1,0:T(8,128)} %get-tuple-element.18), channel_id=1, source_target_pairs={{0,1},{1,0},{2,3},{3,2},{4,5},{5,4},{6,7},{7,6},{8,9},{9,8},{10,11... | collective-permute-start | bytes 5898248 | tf_op jit(solution)/shard_map/ppermute | solution.py:193
  27.4 2.3 %collective-permute-start = (f32[256,640]{1,0:T(8,128)}, f32[256,640]{1,0:T(8,128)S(1)}, u32[]{:S(2)}, u32[]{:S(2)}) collective-permute-start(f32[256,640]{1,0:T(8,128)} %get-tuple-element.16), channel_id=1, source_target_pairs={{0,1},{1,0},{2,3},{3,2},{4,5},{5,4},{6,7},{7,6},{8,9},{9,8},{10,11... | collective-permute-start | bytes 1966088 | tf_op jit(solution)/shard_map/ppermute | solution.py:193
  30.8 18.0 %collective-permute-start.1 = (f32[256,640]{1,0:T(8,128)S(1)}, f32[256,640]{1,0:T(8,128)S(1)}, u32[]{:S(2)}, u32[]{:S(2)}) collective-permute-start(f32[256,640]{1,0:T(8,128)S(1)} %add.28.own_ref), channel_id=1, source_target_pairs={{0,2},{1,3},{2,0},{3,1},{4,6},{5,7},{6,4},{7,5},{8,10},{9,11},{10,... | collective-permute-start | bytes 1966088 | tf_op jit(solution)/shard_map/ppermute | solution.py:193
  33.8 16.7 %collective-permute-start.5 = (f32[768,128]{1,0:T(8,128)S(1)}, f32[768,128]{1,0:T(8,128)S(1)}, u32[]{:S(2)}, u32[]{:S(2)}) collective-permute-start(f32[768,128]{1,0:T(8,128)S(1)} %slice.132), channel_id=1, source_target_pairs={{0,1},{1,0},{2,3},{3,2},{4,5},{5,4},{6,7},{7,6},{8,9},{9,8},{10,11... | collective-permute-start | bytes 1179656 | tf_op jit(solution)/shard_map/ppermute | solution.py:193
  34.0 17.2 %collective-permute-start.2 = (f32[256,128]{1,0:T(8,128)S(1)}, f32[256,128]{1,0:T(8,128)S(1)}, u32[]{:S(2)}, u32[]{:S(2)}) collective-permute-start(f32[256,128]{1,0:T(8,128)S(1)} %slice.128), channel_id=1, source_target_pairs={{0,1},{1,0},{2,3},{3,2},{4,5},{5,4},{6,7},{7,6},{8,9},{9,8},{10,11... | collective-permute-start | bytes 393224 | tf_op jit(solution)/shard_map/ppermute | solution.py:193
  48.8 2.3 %collective-permute-start.3 = (f32[256,128]{1,0:T(8,128)S(1)}, f32[256,128]{1,0:T(8,128)S(1)}, u32[]{:S(2)}, u32[]{:S(2)}) collective-permute-start(f32[256,128]{1,0:T(8,128)S(1)} %slice.129), channel_id=1, source_target_pairs={{0,1},{1,0},{2,3},{3,2},{4,5},{5,4},{6,7},{7,6},{8,9},{9,8},{10,11... | collective-permute-start | bytes 393224 | tf_op jit(solution)/shard_map/ppermute | solution.py:193
  58.2 14.5 %collective-permute-start.6 = (f32[256,512]{1,0:T(8,128)}, f32[256,512]{1,0:T(8,128)S(1)}, u32[]{:S(2)}, u32[]{:S(2)}) collective-permute-start(f32[256,512]{1,0:T(8,128)} %get-tuple-element.19), channel_id=1, source_target_pairs={{0,2},{1,3},{2,0},{3,1},{4,6},{5,7},{6,4},{7,5},{8,10},{9,11},{10,... | collective-permute-start | bytes 1572872 | tf_op jit(solution)/shard_map/ppermute | solution.py:193
  72.8 14.4 %collective-permute-start.7 = (f32[256,512]{1,0:T(8,128)S(1)}, f32[256,512]{1,0:T(8,128)S(1)}, u32[]{:S(2)}, u32[]{:S(2)}) collective-permute-start(f32[256,512]{1,0:T(8,128)S(1)} %add.30.own_ref), channel_id=1, source_target_pairs={{0,4},{1,5},{2,6},{3,7},{4,0},{5,1},{6,2},{7,3},{8,12},{9,13},{10,... | collective-permute-start | bytes 1572872 | tf_op jit(solution)/shard_map/ppermute | solution.py:193
  75.7 11.6 %collective-permute-start.10 = (f32[512,128]{1,0:T(8,128)S(1)}, f32[512,128]{1,0:T(8,128)S(1)}, u32[]{:S(2)}, u32[]{:S(2)}) collective-permute-start(f32[512,128]{1,0:T(8,128)S(1)} %pad_maximum_fusion), channel_id=1, source_target_pairs={{0,1},{1,0},{2,3},{3,2},{4,5},{5,4},{6,7},{7,6},{8,9},{9,8},{10,11... | collective-permute-start | bytes 786440 | tf_op jit(solution)/shard_map/ppermute | solution.py:193
  76.6 11.5 %collective-permute-start.8 = (f32[256,128]{1,0:T(8,128)S(1)}, f32[256,128]{1,0:T(8,128)S(1)}, u32[]{:S(2)}, u32[]{:S(2)}) collective-permute-start(f32[256,128]{1,0:T(8,128)S(1)} %slice.134), channel_id=1, source_target_pairs={{0,1},{1,0},{2,3},{3,2},{4,5},{5,4},{6,7},{7,6},{8,9},{9,8},{10,11... | collective-permute-start | bytes 393224 | tf_op jit(solution)/shard_map/ppermute | solution.py:193
  95.4 8.0 %collective-permute-start.11 = (f32[256,384]{1,0:T(8,128)}, f32[256,384]{1,0:T(8,128)S(1)}, u32[]{:S(2)}, u32[]{:S(2)}) collective-permute-start(f32[256,384]{1,0:T(8,128)} %get-tuple-element.21), channel_id=1, source_target_pairs={{0,2},{1,5},{2,0},{3,7},{4,6},{5,1},{6,4},{7,3},{8,10},{9,13},{10,... | collective-permute-start | bytes 1179656 | tf_op jit(solution)/shard_map/ppermute | solution.py:193
  104.4 7.8 %collective-permute-start.12 = (f32[256,384]{1,0:T(8,128)S(1)}, f32[256,384]{1,0:T(8,128)S(1)}, u32[]{:S(2)}, u32[]{:S(2)}) collective-permute-start(f32[256,384]{1,0:T(8,128)S(1)} %add.31), channel_id=1, source_target_pairs={{0,4},{1,3},{2,6},{3,1},{4,0},{5,7},{6,2},{7,5},{8,12},{9,11},{10,... | collective-permute-start | bytes 1179656 | tf_op jit(solution)/shard_map/ppermute | solution.py:193
  112.3 9.5 %collective-permute-start.13 = (f32[256,384]{1,0:T(8,128)S(1)}, f32[256,384]{1,0:T(8,128)S(1)}, u32[]{:S(2)}, u32[]{:S(2)}) collective-permute-start(f32[256,384]{1,0:T(8,128)S(1)} %add.32.own_ref), channel_id=1, source_target_pairs={{0,8},{1,9},{2,10},{3,11},{4,12},{5,13},{6,14},{7,15},{8,0},{9,1},... | collective-permute-start | bytes 1179656 | tf_op jit(solution)/shard_map/ppermute | solution.py:193
  113.0 9.7 %collective-permute-start.16 = (f32[256,128]{1,0:T(8,128)S(1)}, f32[256,128]{1,0:T(8,128)S(1)}, u32[]{:S(2)}, u32[]{:S(2)}) collective-permute-start(f32[256,128]{1,0:T(8,128)S(1)} %slice.151.col_ref), channel_id=1, source_target_pairs={{0,1},{1,0},{2,3},{3,2},{4,5},{5,4},{6,7},{7,6},{8,9},{9,8},{10,11... | collective-permute-start | bytes 393224 | tf_op jit(solution)/shard_map/ppermute | solution.py:193
  113.1 9.6 %collective-permute-start.14 = (f32[256,128]{1,0:T(8,128)S(1)}, f32[256,128]{1,0:T(8,128)S(1)}, u32[]{:S(2)}, u32[]{:S(2)}) collective-permute-start(f32[256,128]{1,0:T(8,128)S(1)} %slice.146), channel_id=1, source_target_pairs={{0,1},{1,0},{2,3},{3,2},{4,5},{5,4},{6,7},{7,6},{8,9},{9,8},{10,11... | collective-permute-start | bytes 393224 | tf_op jit(solution)/shard_map/ppermute | solution.py:193
  129.2 6.6 %collective-permute-start.17 = (f32[256,256]{1,0:T(8,128)}, f32[256,256]{1,0:T(8,128)S(1)}, u32[]{:S(2)}, u32[]{:S(2)}) collective-permute-start(f32[256,256]{1,0:T(8,128)} %get-tuple-element.23), channel_id=1, source_target_pairs={{0,2},{1,5},{2,0},{3,7},{4,6},{5,1},{6,4},{7,3},{8,10},{9,13},{10,... | collective-permute-start | bytes 786440 | tf_op jit(solution)/shard_map/ppermute | solution.py:193
  136.8 6.4 %collective-permute-start.18 = (f32[256,256]{1,0:T(8,128)S(1)}, f32[256,256]{1,0:T(8,128)S(1)}, u32[]{:S(2)}, u32[]{:S(2)}) collective-permute-start(f32[256,256]{1,0:T(8,128)S(1)} %add.33), channel_id=1, source_target_pairs={{0,4},{1,9},{2,6},{3,11},{4,0},{5,13},{6,2},{7,15},{8,12},{9,1},{1... | collective-permute-start | bytes 786440 | tf_op jit(solution)/shard_map/ppermute | solution.py:193
  143.2 6.4 %collective-permute-start.19 = (f32[256,256]{1,0:T(8,128)S(1)}, f32[256,256]{1,0:T(8,128)S(1)}, u32[]{:S(2)}, u32[]{:S(2)}) collective-permute-start(f32[256,256]{1,0:T(8,128)S(1)} %add.34), channel_id=1, source_target_pairs={{0,8},{1,3},{2,10},{3,1},{4,12},{5,7},{6,14},{7,5},{8,0},{9,11},{1... | collective-permute-start | bytes 786440 | tf_op jit(solution)/shard_map/ppermute | solution.py:193
  143.6 19.0 %collective-permute-start.25 = (f32[256,384]{1,0:T(8,128)S(1)}, f32[256,384]{1,0:T(8,128)S(1)}, u32[]{:S(2)}, u32[]{:S(2)}) collective-permute-start(f32[256,384]{1,0:T(8,128)S(1)} %slice.127), channel_id=1, source_target_pairs={{0,1},{1,0},{2,3},{3,2},{4,5},{5,4},{6,7},{7,6},{8,9},{9,8},{10,11... | collective-permute-start | bytes 1179656 | tf_op jit(solution)/shard_map/ppermute | solution.py:193
  149.7 12.8 %collective-permute-start.20 = (f32[256,256]{1,0:T(8,128)S(1)}, f32[256,256]{1,0:T(8,128)S(1)}, u32[]{:S(2)}, u32[]{:S(2)}) collective-permute-start(f32[256,256]{1,0:T(8,128)S(1)} %add.35.own_ref), channel_id=1, source_target_pairs={{0,16},{1,17},{2,18},{3,19},{4,20},{5,21},{6,22},{7,23},{8,24},{9,... | collective-permute-start | bytes 786440 | tf_op jit(solution)/shard_map/ppermute | solution.py:193
  152.6 10.1 %collective-permute-start.24 = (f32[256,256]{1,0:T(8,128)S(1)}, f32[256,256]{1,0:T(8,128)S(1)}, u32[]{:S(2)}, u32[]{:S(2)}) collective-permute-start(f32[256,256]{1,0:T(8,128)S(1)} %slice.126), channel_id=1, source_target_pairs={{0,1},{1,0},{2,3},{3,2},{4,5},{5,4},{6,7},{7,6},{8,9},{9,8},{10,11... | collective-permute-start | bytes 786440 | tf_op jit(solution)/shard_map/ppermute | solution.py:193
  152.7 10.0 %collective-permute-start.23 = (f32[256,128]{1,0:T(8,128)S(1)}, f32[256,128]{1,0:T(8,128)S(1)}, u32[]{:S(2)}, u32[]{:S(2)}) collective-permute-start(f32[256,128]{1,0:T(8,128)S(1)} %slice.125), channel_id=1, source_target_pairs={{0,1},{1,0},{2,3},{3,2},{4,5},{5,4},{6,7},{7,6},{8,9},{9,8},{10,11... | collective-permute-start | bytes 393224 | tf_op jit(solution)/shard_map/ppermute | solution.py:193
  153.3 9.5 %collective-permute-start.21 = (f32[256,128]{1,0:T(8,128)S(1)}, f32[256,128]{1,0:T(8,128)S(1)}, u32[]{:S(2)}, u32[]{:S(2)}) collective-permute-start(f32[256,128]{1,0:T(8,128)S(1)} %slice.152), channel_id=1, source_target_pairs={{0,1},{1,0},{2,3},{3,2},{4,5},{5,4},{6,7},{7,6},{8,9},{9,8},{10,11... | collective-permute-start | bytes 393224 | tf_op jit(solution)/shard_map/ppermute | solution.py:193
  170.8 2.1 %collective-permute-start.26 = (f32[1024,128]{1,0:T(8,128)}, f32[1024,128]{1,0:T(8,128)S(1)}, u32[]{:S(2)}, u32[]{:S(2)}) collective-permute-start(f32[1024,128]{1,0:T(8,128)} %shard_map.42.w_ref), channel_id=1, source_target_pairs={{0,1},{1,0},{2,3},{3,2},{4,5},{5,4},{6,7},{7,6},{8,9},{9,8},{10,11... | collective-permute-start | bytes 1572872 | tf_op jit(solution)/shard_map/ppermute | solution.py:193
  (31 other events, 160.0 us)
where the time goes:
time: 182 us
  waiting for transfers between devices  87.9 us (48%)
  Pallas kernels  58.1 us (32%)
  starting transfers between devices  20.7 us (11%)
  local copies, waits for them, and re-layouts  8.25 us (5%)
  other arithmetic  4.5 us (2%)
  matrix products  2.01 us (1%)
    ppermute x27, waiting for transfers between devices, swap(): return lax.ppermute(block, AXES, route)  87.9 us
    pallas_call x2, Pallas kernels, gram(): pl.pallas_call(gram_kernel, grid=(rows // tile,), out_shape=(shape, shape...  26.9 us
    pallas_call x4, Pallas kernels, small_call(): pl.pallas_call(kernel, out_shape=shapes, in_specs=[pl.BlockSpec(memory_sp...  23 us
    ppermute x27, starting transfers between devices, swap(): return lax.ppermute(block, AXES, route)  20.7 us
    pallas_call x1, Pallas kernels, apply(): pl.pallas_call(apply_kernel, grid=(rows // tile,), out_shape=jax.ShapeDty...  8.16 us
    unnamed x56, local copies, waits for them, and re-layouts  4.24 us
  transfers between devices with their start and end apart: 27, of which 15 were waited for; matrix products, arithmetic and copies ran while one was open for 5% of the time, Pallas kernels for 5%

commit v1 on v0

--- a/solution.py
+++ b/solution.py
@@ -47,12 +47,11 @@
     stacked = []
     for j in range(u_ref.shape[0] + 1):
         high, low = split(b_ref[...] if j == 0 else u_ref[j - 1])
-        stacked.append(jnp.concatenate([high, low, high], axis=0))
+        stacked.append((high, low))
     for k in range(levels):
-        high, low = split(v_ref[k])
-        rows = jnp.concatenate([high, high, low], axis=0).T
-        for j, block in enumerate(stacked):
-            product = dot(rows, block)
+        high, low = split(v_ref[k].T)
+        for j, (block_high, block_low) in enumerate(stacked):
+            product = dot(high, block_high) + (dot(high, block_low) + dot(low, block_high))
             place = (pl.ds(k * rank, rank), pl.ds(j * half, half))
             acc[(0,) + place] += product[:, :half]
             acc[(1,) + place] += product[:, half:]
@@ -117,7 +116,7 @@
     answer = solve_values(parity, own_ref, sib_ref, own_other_ref, sib_other_ref)
     z_ref[...] = answer
     column = joined(parity, col_ref[...], col_other_ref[...])
-    next_ref[...] = row_ref[...] - mm(column, answer)
+    next_ref[...] = row_ref[:, : answer.shape[1]] - mm(column, answer)
 
 
 def top_kernel(count, par_ref, own_ref, sib_ref, own_other_ref, sib_other_ref, *refs):
@@ -200,26 +199,60 @@
     tile = min(512, row_count)
     parity = (lax.axis_index(AXES) & 1).reshape(1)
 
-    top, top_other = gram(parity, v, b, u, levels - 1, 1, tile)
-    low, low_other = gram(parity, v, b, u, 0, levels - 1, tile)
-    top = top + swap(top_other, 0, 0)
-    low = low + swap(low_other, 0, 0)
-    rows = [low[k * rank : (k + 1) * rank] for k in range(levels - 1)] + [top]
-
+    own, own_far = gram(parity, v, b, u, levels - 1, 1, tile)
+    own = own + swap(own_far, 0, 0)
+    later, own = lax.optimization_barrier((parity, own))
+    middle, middle_far = gram(later, v, b, u, levels - 2, 1, tile)
+    rows = [None] * levels
     answers, answers_other = [None] * levels, [None] * levels
+    low = None
     for k in range(levels - 1, -1, -1):
         width = (k + 1) * half
         sibling = depth - 1 - k
-        own = rows[k][:, : width + half]
-        for step in range(1, sibling):
-            own = own + swap(own, step, step % (sibling - 1) + 1)
-        sib = swap(own, sibling, sibling)
+        if k < levels - 1:
+            own = rows[k]
+        if k == levels - 2:
+            later, own = lax.optimization_barrier((parity, own))
+            low, low_far = gram(later, v, b, u, 0, levels - 2, tile)
+        if sibling == 2:
+            cut = rank * 2 // 3 // 8 * 8
+            early, late = own[:cut], own[cut:]
+            early_pair, late_far = swap(early, 1, 1), swap(late, 2, 2)
+            if k == levels - 2:
+                early_pair, late_far, low_far = lax.optimization_barrier((early_pair, late_far, low_far))
+            early = early + early_pair
+            both = swap(jnp.concatenate([late, late_far], axis=0), 1, 1)
+            early_far = swap(early, 2, 2)
+            own = jnp.concatenate([early, late + both[: rank - cut]], axis=0)
+            sib = jnp.concatenate([early_far, late_far + both[rank - cut :]], axis=0)
+        else:
+            for step in range(1, sibling):
+                moved = swap(own, step, step % (sibling - 1) + 1)
+                if k == levels - 2 and step == 1:
+                    moved, low_far = lax.optimization_barrier((moved, low_far))
+                own = own + moved
+            sib = swap(own, sibling, sibling)
         own_other = swap(own[:, width:], 0, 0)
+        if k == levels - 1:
+            sib, middle_far = lax.optimization_barrier((sib, middle_far))
+            middle = middle + swap(middle_far, 0, 0)
+            rows[k - 1] = middle
+        if k == levels - 2:
+            low = low + swap(low_far, 0, 0)
+            column = low[:, (k + 2) * half :]
+            column = joined(parity[0], column, swap(column, 0, 0))
+            z = answers[k + 1]
+            low = low[:, : (k + 2) * half] - jnp.dot(
+                column, z, precision=lax.Precision.HIGH, preferred_element_type=F32
+            )
+            for i in range(k):
+                rows[i] = low[i * rank : (i + 1) * rank]
         sib_other = swap(sib[:, width:], 0, 0)
         if k > 0:
-            cols = jnp.concatenate([rows[i][:, width : width + half] for i in range(k)], axis=0)
+            near = [k - 1] if k == levels - 1 else list(range(k))
+            cols = jnp.concatenate([rows[i][:, width : width + half] for i in near], axis=0)
             cols_other = swap(cols, 0, 0)
-            last = slice((k - 1) * rank, k * rank)
+            last = slice((len(near) - 1) * rank, len(near) * rank)
             shape = jax.ShapeDtypeStruct((rank, width), F32)
             z, following = small_call(
                 solve_kernel, (shape, shape), parity, own, sib, own_other, sib_other,
@@ -228,7 +261,7 @@
             answers[k] = z
             answers_other[k] = swap(z[:, half:], 0, 0)
             rows[k - 1] = following
-            if k > 1:
+            if len(near) > 1:
                 before = slice(0, (k - 1) * rank)
                 column = joined(parity[0], cols[before], cols_other[before])
                 change = jnp.dot(column, z, precision=lax.Precision.HIGH, preferred_element_type=F32)

time: 182 us -> 171 us (0.940)
  waiting for transfers between devices: 87.9 us -> 65.5 us
  Pallas kernels: 58.1 us -> 63.3 us
  other arithmetic: 4.5 us -> 8.5 us
  starting transfers between devices: 20.7 us -> 23.3 us
    ppermute x27 -> x31, waiting for transfers between devices: 87.9 us -> 65.5 us  [swap(): return lax.ppermute(block, AXES, route)]
    pallas_call x2 -> x3, Pallas kernels: 26.9 us -> 31.3 us  [gram(): pl.pallas_call(gram_kernel, grid=(rows // tile,), out_shape=(shape, shape...]
    ppermute x27 -> x31, starting transfers between devices: 20.7 us -> 23.3 us  [swap(): return lax.ppermute(block, AXES, route)]
    add x8 -> x10, other arithmetic: 3.56 us -> 5.99 us  [the longest x5 2.13 us: local(): own = own + moved]
    unnamed x56 -> x54, local copies, waits for them, and re-layouts: 4.24 us -> 4.02 us
  transfers between devices with their start and end apart: 27 -> 31, of which waited for: 15 -> 16; matrix products, arithmetic and copies ran while one was open for 5% -> 5% of each run, Pallas kernels for 5% -> 13%
where the time goes in v1:
time: 171 us
  waiting for transfers between devices  65.5 us (38%)
  Pallas kernels  63.3 us (37%)
  starting transfers between devices  23.3 us (14%)
  local copies, waits for them, and re-layouts  8.6 us (5%)
  other arithmetic  8.5 us (5%)
    ppermute x31, waiting for transfers between devices, swap(): return lax.ppermute(block, AXES, route)  65.5 us
    pallas_call x3, Pallas kernels, gram(): pl.pallas_call(gram_kernel, grid=(rows // tile,), out_shape=(shape, shape...  31.3 us
    pallas_call x4, Pallas kernels, small_call(): pl.pallas_call(kernel, out_shape=shapes, in_specs=[pl.BlockSpec(memory_sp...  23.8 us
    ppermute x31, starting transfers between devices, swap(): return lax.ppermute(block, AXES, route)  23.3 us
    pallas_call x1, Pallas kernels, apply(): pl.pallas_call(apply_kernel, grid=(rows // tile,), out_shape=jax.ShapeDty...  8.15 us
    unnamed x54, local copies, waits for them, and re-layouts  4.02 us
  transfers between devices with their start and end apart: 31, of which 16 were waited for; matrix products, arithmetic and copies ran while one was open for 5% of the time, Pallas kernels for 13%

profile of v1, /device:TPU:0, one launch (start us, length us, event | category | flops | bytes accessed | tf_op | source)
XLA Modules:
  0.0 170.7 jit_solution(17750115807024510474)
XLA Ops:
  0.0 9.1 %shard_map.37 = (f32[256,640]{1,0:T(8,128)}, f32[256,640]{1,0:T(8,128)}) custom-call(s32[1]{0:T(128)} %bitcast.par_ref, f32[4,2048,256]{2,1,0:T(8,128)} %v_ref.5, f32[2048,256]{1,0:T(8,128)} %b_ref.7, f32[4,2048,256]{2,1,0:T(8,128)} %u_ref.7), custom_call_target="tpu_custom_call" | custom-call | flops 4026531840 | bytes 13893632 | tf_op jit(solution)/shard_map/pallas_call | solution.py:70
  9.6 1.9 %collective-permute-done = f32[256,640]{1,0:T(8,128)S(1)} collective-permute-done((f32[256,640]{1,0:T(8,128)}, f32[256,640]{1,0:T(8,128)S(1)}, u32[]{:S(2)}, u32[]{:S(2)}) %collective-permute-start) | collective-permute-done | bytes 655392 | tf_op jit(solution)/shard_map/ppermute | solution.py:192
  12.7 2.9 %collective-permute-start.1 = (f32[256,640]{1,0:T(8,128)S(1)}, f32[256,640]{1,0:T(8,128)S(1)}, u32[]{:S(2)}, u32[]{:S(2)}) collective-permute-start(f32[256,640]{1,0:T(8,128)S(1)} %add.37.own_ref), channel_id=1, source_target_pairs={{0,2},{1,3},{2,0},{3,1},{4,6},{5,7},{6,4},{7,5},{8,10},{9,11},{10,... | collective-permute-start | bytes 1966088 | tf_op jit(solution)/shard_map/ppermute | solution.py:192
  15.6 9.1 %shard_map.38 = (f32[256,640]{1,0:T(8,128)}, f32[256,640]{1,0:T(8,128)}) custom-call(s32[1]{0:T(128)} %bitcast.par_ref, f32[4,2048,256]{2,1,0:T(8,128)} %v_ref.5, f32[2048,256]{1,0:T(8,128)} %b_ref.7, f32[4,2048,256]{2,1,0:T(8,128)} %u_ref.7), custom_call_target="tpu_custom_call" | custom-call | flops 4026531840 | bytes 13893632 | tf_op jit(solution)/shard_map/pallas_call | solution.py:70
  24.7 6.0 %collective-permute-done.1.sib_ref = f32[256,640]{1,0:T(8,128)S(1)} collective-permute-done((f32[256,640]{1,0:T(8,128)S(1)}, f32[256,640]{1,0:T(8,128)S(1)}, u32[]{:S(2)}, u32[]{:S(2)}) %collective-permute-start.1) | collective-permute-done | bytes 655392 | tf_op jit(solution)/shard_map/ppermute | solution.py:192
  36.6 6.6 %shard_map.39 = (f32[256,512]{1,0:T(8,128)}, f32[256,512]{1,0:T(8,128)}) custom-call(s32[1]{0:T(128)} %bitcast.par_ref, f32[256,640]{1,0:T(8,128)} %copy-done.4, f32[256,640]{1,0:T(8,128)} %copy-done.13, f32[256,128]{1,0:T(8,128)} %copy-done.19, f32[256,128]{1,0:T(8,128)} %copy-done.20, f32[256,512]{1,0:T(8,128)} %slice.115.row_ref, f32[256,128]{1,0:T(8,128)} %copy-done.9, ...), custom_call_target="tpu_custom_call" | custom-call | flops 3000000000 | bytes 4000000 | tf_op jit(solution)/shard_map/pallas_call | solution.py:141
  45.1 1.8 %collective-permute-start.6 = (f32[168,512]{1,0:T(8,128)S(1)}, f32[168,512]{1,0:T(8,128)S(1)}, u32[]{:S(2)}, u32[]{:S(2)}) collective-permute-start(f32[168,512]{1,0:T(8,128)S(1)} %slice.92), channel_id=1, source_target_pairs={{0,2},{1,3},{2,0},{3,1},{4,6},{5,7},{6,4},{7,5},{8,10},{9,11},{10,... | collective-permute-start | bytes 1032200 | tf_op jit(solution)/shard_map/ppermute | solution.py:192
  47.6 13.1 %shard_map.40 = (f32[512,640]{1,0:T(8,128)}, f32[512,640]{1,0:T(8,128)}) custom-call(s32[1]{0:T(128)} %bitcast.par_ref, f32[4,2048,256]{2,1,0:T(8,128)} %v_ref.5, f32[2048,256]{1,0:T(8,128)} %b_ref.7, f32[4,2048,256]{2,1,0:T(8,128)} %u_ref.7), custom_call_target="tpu_custom_call" | custom-call | flops 8053063680 | bytes 17301504 | tf_op jit(solution)/shard_map/pallas_call | solution.py:70
  65.9 5.8 %collective-permute-done.8 = f32[176,512]{1,0:T(8,128)S(1)} collective-permute-done((f32[176,512]{1,0:T(8,128)S(1)}, f32[176,512]{1,0:T(8,128)S(1)}, u32[]{:S(2)}, u32[]{:S(2)}) %collective-permute-start.8) | collective-permute-done | bytes 360480 | tf_op jit(solution)/shard_map/ppermute | solution.py:192
  77.2 6.0 %shard_map.41 = (f32[256,384]{1,0:T(8,128)}, f32[256,384]{1,0:T(8,128)}) custom-call(s32[1]{0:T(128)} %bitcast.par_ref, f32[256,512]{1,0:T(8,128)} %pad_maximum_fusion.own_ref, f32[256,512]{1,0:T(8,128)} %pad_maximum_fusion.1.sib_ref, f32[256,128]{1,0:T(8,128)} %copy-done.22, f32[256,128]{1,0:T(8,128)} %copy-done.16, f32[256,384]{1,0:T(8,128)} %slice.125.row_ref, ...), custom_call_target="tpu_custom_call" | custom-call | flops 3000000000 | bytes 4000000 | tf_op jit(solution)/shard_map/pallas_call | solution.py:141
  84.7 6.6 %collective-permute-done.15 = f32[256,384]{1,0:T(8,128)S(1)} collective-permute-done((f32[256,384]{1,0:T(8,128)}, f32[256,384]{1,0:T(8,128)S(1)}, u32[]{:S(2)}, u32[]{:S(2)}) %collective-permute-start.15) | collective-permute-done | bytes 393248 | tf_op jit(solution)/shard_map/ppermute | solution.py:192
  93.7 6.4 %collective-permute-done.16 = f32[256,384]{1,0:T(8,128)S(1)} collective-permute-done((f32[256,384]{1,0:T(8,128)S(1)}, f32[256,384]{1,0:T(8,128)S(1)}, u32[]{:S(2)}, u32[]{:S(2)}) %collective-permute-start.16) | collective-permute-done | bytes 393248 | tf_op jit(solution)/shard_map/ppermute | solution.py:192
  100.2 2.5 %collective-permute-start.17 = (f32[256,384]{1,0:T(8,128)S(1)}, f32[256,384]{1,0:T(8,128)S(1)}, u32[]{:S(2)}, u32[]{:S(2)}) collective-permute-start(f32[256,384]{1,0:T(8,128)S(1)} %add.44.own_ref), channel_id=1, source_target_pairs={{0,8},{1,9},{2,10},{3,11},{4,12},{5,13},{6,14},{7,15},{8,0},{9,1},... | collective-permute-start | bytes 1179656 | tf_op jit(solution)/shard_map/ppermute | solution.py:192
  103.8 7.0 %collective-permute-done.17.sib_ref = f32[256,384]{1,0:T(8,128)S(1)} collective-permute-done((f32[256,384]{1,0:T(8,128)S(1)}, f32[256,384]{1,0:T(8,128)S(1)}, u32[]{:S(2)}, u32[]{:S(2)}) %collective-permute-start.17) | collective-permute-done | bytes 393248 | tf_op jit(solution)/shard_map/ppermute | solution.py:192
  113.0 5.1 %shard_map.42 = (f32[256,256]{1,0:T(8,128)}, f32[256,256]{1,0:T(8,128)}) custom-call(s32[1]{0:T(128)} %bitcast.par_ref, f32[256,384]{1,0:T(8,128)} %copy-done.5, f32[256,384]{1,0:T(8,128)} %copy-done.12, f32[256,128]{1,0:T(8,128)} %copy-done.24, f32[256,128]{1,0:T(8,128)} %copy-done.26, f32[256,256]{1,0:T(8,128)} %slice.133.row_ref, f32[256,128]{1,0:T(8,128)} %copy-done.8, ...), custom_call_target="tpu_custom_call" | custom-call | flops 3000000000 | bytes 4000000 | tf_op jit(solution)/shard_map/pallas_call | solution.py:141
  119.5 5.1 %collective-permute-done.21 = f32[256,256]{1,0:T(8,128)S(1)} collective-permute-done((f32[256,256]{1,0:T(8,128)}, f32[256,256]{1,0:T(8,128)S(1)}, u32[]{:S(2)}, u32[]{:S(2)}) %collective-permute-start.21) | collective-permute-done | bytes 262176 | tf_op jit(solution)/shard_map/ppermute | solution.py:192
  126.4 5.7 %collective-permute-done.22 = f32[256,256]{1,0:T(8,128)S(1)} collective-permute-done((f32[256,256]{1,0:T(8,128)S(1)}, f32[256,256]{1,0:T(8,128)S(1)}, u32[]{:S(2)}, u32[]{:S(2)}) %collective-permute-start.22) | collective-permute-done | bytes 262176 | tf_op jit(solution)/shard_map/ppermute | solution.py:192
  132.1 1.8 %collective-permute-start.23 = (f32[256,256]{1,0:T(8,128)S(1)}, f32[256,256]{1,0:T(8,128)S(1)}, u32[]{:S(2)}, u32[]{:S(2)}) collective-permute-start(f32[256,256]{1,0:T(8,128)S(1)} %add.46), channel_id=1, source_target_pairs={{0,8},{1,3},{2,10},{3,1},{4,12},{5,7},{6,14},{7,5},{8,0},{9,11},{1... | collective-permute-start | bytes 786440 | tf_op jit(solution)/shard_map/ppermute | solution.py:192
  134.1 4.5 %collective-permute-done.23 = f32[256,256]{1,0:T(8,128)S(1)} collective-permute-done((f32[256,256]{1,0:T(8,128)S(1)}, f32[256,256]{1,0:T(8,128)S(1)}, u32[]{:S(2)}, u32[]{:S(2)}) %collective-permute-start.23) | collective-permute-done | bytes 262176 | tf_op jit(solution)/shard_map/ppermute | solution.py:192
  138.6 2.8 %collective-permute-start.24 = (f32[256,256]{1,0:T(8,128)S(1)}, f32[256,256]{1,0:T(8,128)S(1)}, u32[]{:S(2)}, u32[]{:S(2)}) collective-permute-start(f32[256,256]{1,0:T(8,128)S(1)} %add.47.own_ref), channel_id=1, source_target_pairs={{0,16},{1,17},{2,18},{3,19},{4,20},{5,21},{6,22},{7,23},{8,24},{9,... | collective-permute-start | bytes 786440 | tf_op jit(solution)/shard_map/ppermute | solution.py:192
  142.2 9.2 %collective-permute-done.24.sib_ref = f32[256,256]{1,0:T(8,128)S(1)} collective-permute-done((f32[256,256]{1,0:T(8,128)S(1)}, f32[256,256]{1,0:T(8,128)S(1)}, u32[]{:S(2)}, u32[]{:S(2)}) %collective-permute-start.24) | collective-permute-done | bytes 262176 | tf_op jit(solution)/shard_map/ppermute | solution.py:192
  153.5 6.1 %shard_map.43.w_ref = f32[1024,128]{1,0:T(8,128)} custom-call(s32[1]{0:T(128)} %bitcast.par_ref, f32[256,256]{1,0:T(8,128)} %copy-done.6, f32[256,256]{1,0:T(8,128)} %copy-done.11, f32[256,128]{1,0:T(8,128)} %copy-done.18, f32[256,128]{1,0:T(8,128)} %copy-done.23, f32[256,256]{1,0:T(8,128)} %get-tuple-element.46.refs_0_, ...), custom_call_target="tpu_custom_call" | custom-call | flops 3000000000 | bytes 4000000 | tf_op jit(solution)/shard_map/pallas_call | solution.py:141
  159.7 2.0 %collective-permute-done.30.w_other_ref = f32[1024,128]{1,0:T(8,128)S(1)} collective-permute-done((f32[1024,128]{1,0:T(8,128)}, f32[1024,128]{1,0:T(8,128)S(1)}, u32[]{:S(2)}, u32[]{:S(2)}) %collective-permute-start.30) | collective-permute-done | bytes 524320 | tf_op jit(solution)/shard_map/ppermute | solution.py:192
  162.5 8.2 %shard_map.44 = f32[2048,256]{1,0:T(8,128)} custom-call(s32[1]{0:T(128)} %bitcast.par_ref, f32[2048,256]{1,0:T(8,128)} %b_ref.7, f32[4,2048,256]{2,1,0:T(8,128)} %u_ref.7, f32[1024,128]{1,0:T(8,128)} %shard_map.43.w_ref, f32[1024,128]{1,0:T(8,128)} %copy-done.7), custom_call_target="tpu_custom_call" | custom-call | tf_op jit(solution)/shard_map/pallas_call | solution.py:172
  (137 shorter events, 34.8 us)
Async XLA Ops:
  12.7 18.0 %collective-permute-start.1 = (f32[256,640]{1,0:T(8,128)S(1)}, f32[256,640]{1,0:T(8,128)S(1)}, u32[]{:S(2)}, u32[]{:S(2)}) collective-permute-start(f32[256,640]{1,0:T(8,128)S(1)} %add.37.own_ref), channel_id=1, source_target_pairs={{0,2},{1,3},{2,0},{3,1},{4,6},{5,7},{6,4},{7,5},{8,10},{9,11},{10,... | collective-permute-start | bytes 1966088 | tf_op jit(solution)/shard_map/ppermute | solution.py:192
  30.7 4.6 %collective-permute-start.2 = (f32[256,128]{1,0:T(8,128)S(1)}, f32[256,128]{1,0:T(8,128)S(1)}, u32[]{:S(2)}, u32[]{:S(2)}) collective-permute-start(f32[256,128]{1,0:T(8,128)S(1)} %slice.88), channel_id=1, source_target_pairs={{0,1},{1,0},{2,3},{3,2},{4,5},{5,4},{6,7},{7,6},{8,9},{9,8},{10,11... | collective-permute-start | bytes 393224 | tf_op jit(solution)/shard_map/ppermute | solution.py:192
  31.2 4.0 %collective-permute-start.3 = (f32[256,128]{1,0:T(8,128)S(1)}, f32[256,128]{1,0:T(8,128)S(1)}, u32[]{:S(2)}, u32[]{:S(2)}) collective-permute-start(f32[256,128]{1,0:T(8,128)S(1)} %slice.89), channel_id=1, source_target_pairs={{0,1},{1,0},{2,3},{3,2},{4,5},{5,4},{6,7},{7,6},{8,9},{9,8},{10,11... | collective-permute-start | bytes 393224 | tf_op jit(solution)/shard_map/ppermute | solution.py:192
  45.1 15.6 %collective-permute-start.6 = (f32[168,512]{1,0:T(8,128)S(1)}, f32[168,512]{1,0:T(8,128)S(1)}, u32[]{:S(2)}, u32[]{:S(2)}) collective-permute-start(f32[168,512]{1,0:T(8,128)S(1)} %slice.92), channel_id=1, source_target_pairs={{0,2},{1,3},{2,0},{3,1},{4,6},{5,7},{6,4},{7,5},{8,10},{9,11},{10,... | collective-permute-start | bytes 1032200 | tf_op jit(solution)/shard_map/ppermute | solution.py:192
  46.9 13.8 %collective-permute-start.7 = (f32[88,512]{1,0:T(8,128)S(1)}, f32[88,512]{1,0:T(8,128)S(1)}, u32[]{:S(2)}, u32[]{:S(2)}) collective-permute-start(f32[88,512]{1,0:T(8,128)S(1)} %slice.93), channel_id=1, source_target_pairs={{0,4},{1,5},{2,6},{3,7},{4,0},{5,1},{6,2},{7,3},{8,12},{9,13},{10,... | collective-permute-start | bytes 540680 | tf_op jit(solution)/shard_map/ppermute | solution.py:192
  60.8 3.4 %collective-permute-start.12 = (f32[512,640]{1,0:T(8,128)}, f32[512,640]{1,0:T(8,128)}, u32[]{:S(2)}, u32[]{:S(2)}) collective-permute-start(f32[512,640]{1,0:T(8,128)} %get-tuple-element.41), channel_id=1, source_target_pairs={{0,1},{1,0},{2,3},{3,2},{4,5},{5,4},{6,7},{7,6},{8,9},{9,8},{10,11... | collective-permute-start | bytes 3932168 | tf_op jit(solution)/shard_map/ppermute | solution.py:192
  60.9 10.9 %collective-permute-start.8 = (f32[176,512]{1,0:T(8,128)S(1)}, f32[176,512]{1,0:T(8,128)S(1)}, u32[]{:S(2)}, u32[]{:S(2)}) collective-permute-start(f32[176,512]{1,0:T(8,128)S(1)} %pad_maximum_fusion.2), channel_id=1, source_target_pairs={{0,2},{1,3},{2,0},{3,1},{4,6},{5,7},{6,4},{7,5},{8,10},{9,11},{10,... | collective-permute-start | bytes 1081352 | tf_op jit(solution)/shard_map/ppermute | solution.py:192
  61.5 10.3 %collective-permute-start.9 = (f32[168,512]{1,0:T(8,128)S(1)}, f32[168,512]{1,0:T(8,128)S(1)}, u32[]{:S(2)}, u32[]{:S(2)}) collective-permute-start(f32[168,512]{1,0:T(8,128)S(1)} %slice_add_fusion.2), channel_id=1, source_target_pairs={{0,4},{1,5},{2,6},{3,7},{4,0},{5,1},{6,2},{7,3},{8,12},{9,13},{10,... | collective-permute-start | bytes 1032200 | tf_op jit(solution)/shard_map/ppermute | solution.py:192
  65.7 6.2 %collective-permute-start.13 = (f32[512,128]{1,0:T(8,128)S(1)}, f32[512,128]{1,0:T(8,128)S(1)}, u32[]{:S(2)}, u32[]{:S(2)}) collective-permute-start(f32[512,128]{1,0:T(8,128)S(1)} %slice.124), channel_id=1, source_target_pairs={{0,1},{1,0},{2,3},{3,2},{4,5},{5,4},{6,7},{7,6},{8,9},{9,8},{10,11... | collective-permute-start | bytes 786440 | tf_op jit(solution)/shard_map/ppermute | solution.py:192
  71.8 4.7 %collective-permute-start.11 = (f32[256,128]{1,0:T(8,128)S(1)}, f32[256,128]{1,0:T(8,128)S(1)}, u32[]{:S(2)}, u32[]{:S(2)}) collective-permute-start(f32[256,128]{1,0:T(8,128)S(1)} %fusion.12), channel_id=1, source_target_pairs={{0,1},{1,0},{2,3},{3,2},{4,5},{5,4},{6,7},{7,6},{8,9},{9,8},{10,11... | collective-permute-start | bytes 393224 | tf_op jit(solution)/shard_map/ppermute | solution.py:192
  73.2 3.3 %collective-permute-start.10 = (f32[256,128]{1,0:T(8,128)S(1)}, f32[256,128]{1,0:T(8,128)S(1)}, u32[]{:S(2)}, u32[]{:S(2)}) collective-permute-start(f32[256,128]{1,0:T(8,128)S(1)} %fusion.13), channel_id=1, source_target_pairs={{0,1},{1,0},{2,3},{3,2},{4,5},{5,4},{6,7},{7,6},{8,9},{9,8},{10,11... | collective-permute-start | bytes 393224 | tf_op jit(solution)/shard_map/ppermute | solution.py:192
  83.3 8.0 %collective-permute-start.15 = (f32[256,384]{1,0:T(8,128)}, f32[256,384]{1,0:T(8,128)S(1)}, u32[]{:S(2)}, u32[]{:S(2)}) collective-permute-start(f32[256,384]{1,0:T(8,128)} %get-tuple-element.43), channel_id=1, source_target_pairs={{0,2},{1,5},{2,0},{3,7},{4,6},{5,1},{6,4},{7,3},{8,10},{9,13},{10,... | collective-permute-start | bytes 1179656 | tf_op jit(solution)/shard_map/ppermute | solution.py:192
  92.3 7.8 %collective-permute-start.16 = (f32[256,384]{1,0:T(8,128)S(1)}, f32[256,384]{1,0:T(8,128)S(1)}, u32[]{:S(2)}, u32[]{:S(2)}) collective-permute-start(f32[256,384]{1,0:T(8,128)S(1)} %add.43), channel_id=1, source_target_pairs={{0,4},{1,3},{2,6},{3,1},{4,0},{5,7},{6,2},{7,5},{8,12},{9,11},{10,... | collective-permute-start | bytes 1179656 | tf_op jit(solution)/shard_map/ppermute | solution.py:192
  100.2 10.5 %collective-permute-start.17 = (f32[256,384]{1,0:T(8,128)S(1)}, f32[256,384]{1,0:T(8,128)S(1)}, u32[]{:S(2)}, u32[]{:S(2)}) collective-permute-start(f32[256,384]{1,0:T(8,128)S(1)} %add.44.own_ref), channel_id=1, source_target_pairs={{0,8},{1,9},{2,10},{3,11},{4,12},{5,13},{6,14},{7,15},{8,0},{9,1},... | collective-permute-start | bytes 1179656 | tf_op jit(solution)/shard_map/ppermute | solution.py:192
  103.1 8.5 %collective-permute-start.20 = (f32[256,128]{1,0:T(8,128)S(1)}, f32[256,128]{1,0:T(8,128)S(1)}, u32[]{:S(2)}, u32[]{:S(2)}) collective-permute-start(f32[256,128]{1,0:T(8,128)S(1)} %slice.134.col_ref), channel_id=1, source_target_pairs={{0,1},{1,0},{2,3},{3,2},{4,5},{5,4},{6,7},{7,6},{8,9},{9,8},{10,11... | collective-permute-start | bytes 393224 | tf_op jit(solution)/shard_map/ppermute | solution.py:192
  103.2 8.4 %collective-permute-start.18 = (f32[256,128]{1,0:T(8,128)S(1)}, f32[256,128]{1,0:T(8,128)S(1)}, u32[]{:S(2)}, u32[]{:S(2)}) collective-permute-start(f32[256,128]{1,0:T(8,128)S(1)} %slice.128), channel_id=1, source_target_pairs={{0,1},{1,0},{2,3},{3,2},{4,5},{5,4},{6,7},{7,6},{8,9},{9,8},{10,11... | collective-permute-start | bytes 393224 | tf_op jit(solution)/shard_map/ppermute | solution.py:192
  118.1 6.6 %collective-permute-start.21 = (f32[256,256]{1,0:T(8,128)}, f32[256,256]{1,0:T(8,128)S(1)}, u32[]{:S(2)}, u32[]{:S(2)}) collective-permute-start(f32[256,256]{1,0:T(8,128)} %get-tuple-element.45), channel_id=1, source_target_pairs={{0,2},{1,5},{2,0},{3,7},{4,6},{5,1},{6,4},{7,3},{8,10},{9,13},{10,... | collective-permute-start | bytes 786440 | tf_op jit(solution)/shard_map/ppermute | solution.py:192
  125.7 6.4 %collective-permute-start.22 = (f32[256,256]{1,0:T(8,128)S(1)}, f32[256,256]{1,0:T(8,128)S(1)}, u32[]{:S(2)}, u32[]{:S(2)}) collective-permute-start(f32[256,256]{1,0:T(8,128)S(1)} %add.45), channel_id=1, source_target_pairs={{0,4},{1,9},{2,6},{3,11},{4,0},{5,13},{6,2},{7,15},{8,12},{9,1},{1... | collective-permute-start | bytes 786440 | tf_op jit(solution)/shard_map/ppermute | solution.py:192
  132.1 6.4 %collective-permute-start.23 = (f32[256,256]{1,0:T(8,128)S(1)}, f32[256,256]{1,0:T(8,128)S(1)}, u32[]{:S(2)}, u32[]{:S(2)}) collective-permute-start(f32[256,256]{1,0:T(8,128)S(1)} %add.46), channel_id=1, source_target_pairs={{0,8},{1,3},{2,10},{3,1},{4,12},{5,7},{6,14},{7,5},{8,0},{9,11},{1... | collective-permute-start | bytes 786440 | tf_op jit(solution)/shard_map/ppermute | solution.py:192
  134.0 17.5 %collective-permute-start.29 = (f32[256,384]{1,0:T(8,128)S(1)}, f32[256,384]{1,0:T(8,128)S(1)}, u32[]{:S(2)}, u32[]{:S(2)}) collective-permute-start(f32[256,384]{1,0:T(8,128)S(1)} %slice.114), channel_id=1, source_target_pairs={{0,1},{1,0},{2,3},{3,2},{4,5},{5,4},{6,7},{7,6},{8,9},{9,8},{10,11... | collective-permute-start | bytes 1179656 | tf_op jit(solution)/shard_map/ppermute | solution.py:192
  138.6 12.8 %collective-permute-start.24 = (f32[256,256]{1,0:T(8,128)S(1)}, f32[256,256]{1,0:T(8,128)S(1)}, u32[]{:S(2)}, u32[]{:S(2)}) collective-permute-start(f32[256,256]{1,0:T(8,128)S(1)} %add.47.own_ref), channel_id=1, source_target_pairs={{0,16},{1,17},{2,18},{3,19},{4,20},{5,21},{6,22},{7,23},{8,24},{9,... | collective-permute-start | bytes 786440 | tf_op jit(solution)/shard_map/ppermute | solution.py:192
  141.5 10.1 %collective-permute-start.28 = (f32[256,256]{1,0:T(8,128)S(1)}, f32[256,256]{1,0:T(8,128)S(1)}, u32[]{:S(2)}, u32[]{:S(2)}) collective-permute-start(f32[256,256]{1,0:T(8,128)S(1)} %slice.113), channel_id=1, source_target_pairs={{0,1},{1,0},{2,3},{3,2},{4,5},{5,4},{6,7},{7,6},{8,9},{9,8},{10,11... | collective-permute-start | bytes 786440 | tf_op jit(solution)/shard_map/ppermute | solution.py:192
  141.6 10.0 %collective-permute-start.27 = (f32[256,128]{1,0:T(8,128)S(1)}, f32[256,128]{1,0:T(8,128)S(1)}, u32[]{:S(2)}, u32[]{:S(2)}) collective-permute-start(f32[256,128]{1,0:T(8,128)S(1)} %slice.112), channel_id=1, source_target_pairs={{0,1},{1,0},{2,3},{3,2},{4,5},{5,4},{6,7},{7,6},{8,9},{9,8},{10,11... | collective-permute-start | bytes 393224 | tf_op jit(solution)/shard_map/ppermute | solution.py:192
  142.1 9.4 %collective-permute-start.25 = (f32[256,128]{1,0:T(8,128)S(1)}, f32[256,128]{1,0:T(8,128)S(1)}, u32[]{:S(2)}, u32[]{:S(2)}) collective-permute-start(f32[256,128]{1,0:T(8,128)S(1)} %slice.135), channel_id=1, source_target_pairs={{0,1},{1,0},{2,3},{3,2},{4,5},{5,4},{6,7},{7,6},{8,9},{9,8},{10,11... | collective-permute-start | bytes 393224 | tf_op jit(solution)/shard_map/ppermute | solution.py:192
  (34 other events, 148.2 us)

commit v2 on v1

--- a/solution.py
+++ b/solution.py
@@ -93,9 +93,10 @@
     width = own_ref.shape[1] - half
     own_rank = joined(parity, own_ref[:, width:], own_other_ref[...])
     sib_rank = joined(parity, sib_ref[:, width:], sib_other_ref[...])
-    terms = sib_ref[:, :width] - mm(sib_rank, own_ref[:, :width])
-    power = mm(sib_rank, own_rank)
-    answer = terms + mm(power, terms)
+    rank = own_rank.shape[1]
+    products = mm(sib_rank, jnp.concatenate([own_rank, own_ref[:, :width]], axis=1))
+    power = products[:, :rank]
+    answer = sib_ref[:, :width] - products[:, rank:]
 
     def going(state):
         count, size, _, _ = state
@@ -103,11 +104,10 @@
 
     def sweep(state):
         count, _, power, answer = state
-        power = mm(power, power)
-        answer = answer + mm(power, answer)
-        return count + 1, jnp.sum(power * power), power, answer
-
-    state = (jnp.int32(1), jnp.sum(power * power), power, answer)
+        products = mm(power, jnp.concatenate([power, answer], axis=1))
+        return count + 1, jnp.sum(power * power), products[:, :rank], answer + products[:, rank:]
+
+    state = sweep((jnp.int32(0), jnp.float32(0), power, answer))
     return lax.while_loop(going, sweep, state)[3]
 
 

time: 171 us -> 169 us (0.988)
  Pallas kernels: 63.3 us -> 60.7 us
  waiting for transfers between devices: 65.5 us -> 67.7 us
  starting transfers between devices: 23.3 us -> 21.2 us
    pallas_call x4, Pallas kernels: 23.8 us -> 21.2 us  [small_call(): pl.pallas_call(kernel, out_shape=shapes, in_specs=[pl.BlockSpec(memory_sp...]
    ppermute x31, waiting for transfers between devices: 65.5 us -> 67.7 us  [swap(): return lax.ppermute(block, AXES, route)]
    ppermute x31, starting transfers between devices: 23.3 us -> 21.2 us  [swap(): return lax.ppermute(block, AXES, route)]
where the time goes in v2:
time: 169 us; the launch traced here: 168 us
  waiting for transfers between devices  67.7 us (40%)
  Pallas kernels  60.7 us (36%)
  starting transfers between devices  21.2 us (13%)
  local copies, waits for them, and re-layouts  8.6 us (5%)
  other arithmetic  8.5 us (5%)
    ppermute x31, waiting for transfers between devices, swap(): return lax.ppermute(block, AXES, route)  67.7 us
    pallas_call x3, Pallas kernels, gram(): pl.pallas_call(gram_kernel, grid=(rows // tile,), out_shape=(shape, shape...  31.3 us
    pallas_call x4, Pallas kernels, small_call(): pl.pallas_call(kernel, out_shape=shapes, in_specs=[pl.BlockSpec(memory_sp...  21.2 us
    ppermute x31, starting transfers between devices, swap(): return lax.ppermute(block, AXES, route)  21.2 us
    pallas_call x1, Pallas kernels, apply(): pl.pallas_call(apply_kernel, grid=(rows // tile,), out_shape=jax.ShapeDty...  8.15 us
    unnamed x54, local copies, waits for them, and re-layouts  4.02 us
  transfers between devices with their start and end apart: 31, of which 16 were waited for; matrix products, arithmetic and copies ran while one was open for 5% of the time, Pallas kernels for 13%

profile of v2, /device:TPU:0, one launch (start us, length us, event | category | flops | bytes accessed | tf_op | source)
XLA Modules:
  0.0 168.2 jit_solution(12118295454398437388)
XLA Ops:
  0.0 9.1 %shard_map.37 = (f32[256,640]{1,0:T(8,128)}, f32[256,640]{1,0:T(8,128)}) custom-call(s32[1]{0:T(128)} %bitcast.par_ref, f32[4,2048,256]{2,1,0:T(8,128)} %v_ref.5, f32[2048,256]{1,0:T(8,128)} %b_ref.7, f32[4,2048,256]{2,1,0:T(8,128)} %u_ref.7), custom_call_target="tpu_custom_call" | custom-call | flops 4026531840 | bytes 13893632 | tf_op jit(solution)/shard_map/pallas_call | solution.py:70
  9.6 1.9 %collective-permute-done = f32[256,640]{1,0:T(8,128)S(1)} collective-permute-done((f32[256,640]{1,0:T(8,128)}, f32[256,640]{1,0:T(8,128)S(1)}, u32[]{:S(2)}, u32[]{:S(2)}) %collective-permute-start) | collective-permute-done | bytes 655392 | tf_op jit(solution)/shard_map/ppermute | solution.py:192
  12.7 2.9 %collective-permute-start.1 = (f32[256,640]{1,0:T(8,128)S(1)}, f32[256,640]{1,0:T(8,128)S(1)}, u32[]{:S(2)}, u32[]{:S(2)}) collective-permute-start(f32[256,640]{1,0:T(8,128)S(1)} %add.37.own_ref), channel_id=1, source_target_pairs={{0,2},{1,3},{2,0},{3,1},{4,6},{5,7},{6,4},{7,5},{8,10},{9,11},{10,... | collective-permute-start | bytes 1966088 | tf_op jit(solution)/shard_map/ppermute | solution.py:192
  15.6 9.1 %shard_map.38 = (f32[256,640]{1,0:T(8,128)}, f32[256,640]{1,0:T(8,128)}) custom-call(s32[1]{0:T(128)} %bitcast.par_ref, f32[4,2048,256]{2,1,0:T(8,128)} %v_ref.5, f32[2048,256]{1,0:T(8,128)} %b_ref.7, f32[4,2048,256]{2,1,0:T(8,128)} %u_ref.7), custom_call_target="tpu_custom_call" | custom-call | flops 4026531840 | bytes 13893632 | tf_op jit(solution)/shard_map/pallas_call | solution.py:70
  24.7 6.0 %collective-permute-done.1.sib_ref = f32[256,640]{1,0:T(8,128)S(1)} collective-permute-done((f32[256,640]{1,0:T(8,128)S(1)}, f32[256,640]{1,0:T(8,128)S(1)}, u32[]{:S(2)}, u32[]{:S(2)}) %collective-permute-start.1) | collective-permute-done | bytes 655392 | tf_op jit(solution)/shard_map/ppermute | solution.py:192
  36.6 6.0 %shard_map.39 = (f32[256,512]{1,0:T(8,128)}, f32[256,512]{1,0:T(8,128)}) custom-call(s32[1]{0:T(128)} %bitcast.par_ref, f32[256,640]{1,0:T(8,128)} %copy-done.4, f32[256,640]{1,0:T(8,128)} %copy-done.13, f32[256,128]{1,0:T(8,128)} %copy-done.19, f32[256,128]{1,0:T(8,128)} %copy-done.20, f32[256,512]{1,0:T(8,128)} %slice.115.row_ref, f32[256,128]{1,0:T(8,128)} %copy-done.9, ...), custom_call_target="tpu_custom_call" | custom-call | flops 3000000000 | bytes 4000000 | tf_op jit(solution)/shard_map/pallas_call | solution.py:141
  44.5 1.8 %collective-permute-start.6 = (f32[168,512]{1,0:T(8,128)S(1)}, f32[168,512]{1,0:T(8,128)S(1)}, u32[]{:S(2)}, u32[]{:S(2)}) collective-permute-start(f32[168,512]{1,0:T(8,128)S(1)} %slice.92), channel_id=1, source_target_pairs={{0,2},{1,3},{2,0},{3,1},{4,6},{5,7},{6,4},{7,5},{8,10},{9,11},{10,... | collective-permute-start | bytes 1032200 | tf_op jit(solution)/shard_map/ppermute | solution.py:192
  47.9 13.1 %shard_map.40 = (f32[512,640]{1,0:T(8,128)}, f32[512,640]{1,0:T(8,128)}) custom-call(s32[1]{0:T(128)} %bitcast.par_ref, f32[4,2048,256]{2,1,0:T(8,128)} %v_ref.5, f32[2048,256]{1,0:T(8,128)} %b_ref.7, f32[4,2048,256]{2,1,0:T(8,128)} %u_ref.7), custom_call_target="tpu_custom_call" | custom-call | flops 8053063680 | bytes 17301504 | tf_op jit(solution)/shard_map/pallas_call | solution.py:70
  62.1 2.4 %collective-permute-done.12 = f32[512,640]{1,0:T(8,128)} collective-permute-done((f32[512,640]{1,0:T(8,128)}, f32[512,640]{1,0:T(8,128)}, u32[]{:S(2)}, u32[]{:S(2)}) %collective-permute-start.12) | collective-permute-done | bytes 1310752 | tf_op jit(solution)/shard_map/ppermute | solution.py:192
  66.2 5.8 %collective-permute-done.8 = f32[176,512]{1,0:T(8,128)S(1)} collective-permute-done((f32[176,512]{1,0:T(8,128)S(1)}, f32[176,512]{1,0:T(8,128)S(1)}, u32[]{:S(2)}, u32[]{:S(2)}) %collective-permute-start.8) | collective-permute-done | bytes 360480 | tf_op jit(solution)/shard_map/ppermute | solution.py:192
  77.5 5.5 %shard_map.41 = (f32[256,384]{1,0:T(8,128)}, f32[256,384]{1,0:T(8,128)}) custom-call(s32[1]{0:T(128)} %bitcast.par_ref, f32[256,512]{1,0:T(8,128)} %pad_maximum_fusion.own_ref, f32[256,512]{1,0:T(8,128)} %pad_maximum_fusion.1.sib_ref, f32[256,128]{1,0:T(8,128)} %copy-done.22, f32[256,128]{1,0:T(8,128)} %copy-done.16, f32[256,384]{1,0:T(8,128)} %slice.125.row_ref, ...), custom_call_target="tpu_custom_call" | custom-call | flops 3000000000 | bytes 4000000 | tf_op jit(solution)/shard_map/pallas_call | solution.py:141
  84.4 6.5 %collective-permute-done.15 = f32[256,384]{1,0:T(8,128)S(1)} collective-permute-done((f32[256,384]{1,0:T(8,128)}, f32[256,384]{1,0:T(8,128)S(1)}, u32[]{:S(2)}, u32[]{:S(2)}) %collective-permute-start.15) | collective-permute-done | bytes 393248 | tf_op jit(solution)/shard_map/ppermute | solution.py:192
  92.6 7.3 %collective-permute-done.16 = f32[256,384]{1,0:T(8,128)S(1)} collective-permute-done((f32[256,384]{1,0:T(8,128)S(1)}, f32[256,384]{1,0:T(8,128)S(1)}, u32[]{:S(2)}, u32[]{:S(2)}) %collective-permute-start.16) | collective-permute-done | bytes 393248 | tf_op jit(solution)/shard_map/ppermute | solution.py:192
  99.9 1.6 collective-permute-start.17
  102.6 7.1 %collective-permute-done.17.sib_ref = f32[256,384]{1,0:T(8,128)S(1)} collective-permute-done((f32[256,384]{1,0:T(8,128)S(1)}, f32[256,384]{1,0:T(8,128)S(1)}, u32[]{:S(2)}, u32[]{:S(2)}) %collective-permute-start.17) | collective-permute-done | bytes 393248 | tf_op jit(solution)/shard_map/ppermute | solution.py:192
  112.0 4.4 %shard_map.42 = (f32[256,256]{1,0:T(8,128)}, f32[256,256]{1,0:T(8,128)}) custom-call(s32[1]{0:T(128)} %bitcast.par_ref, f32[256,384]{1,0:T(8,128)} %copy-done.5, f32[256,384]{1,0:T(8,128)} %copy-done.12, f32[256,128]{1,0:T(8,128)} %copy-done.24, f32[256,128]{1,0:T(8,128)} %copy-done.26, f32[256,256]{1,0:T(8,128)} %slice.133.row_ref, f32[256,128]{1,0:T(8,128)} %copy-done.8, ...), custom_call_target="tpu_custom_call" | custom-call | flops 3000000000 | bytes 4000000 | tf_op jit(solution)/shard_map/pallas_call | solution.py:141
  117.9 5.1 %collective-permute-done.21 = f32[256,256]{1,0:T(8,128)S(1)} collective-permute-done((f32[256,256]{1,0:T(8,128)}, f32[256,256]{1,0:T(8,128)S(1)}, u32[]{:S(2)}, u32[]{:S(2)}) %collective-permute-start.21) | collective-permute-done | bytes 262176 | tf_op jit(solution)/shard_map/ppermute | solution.py:192
  124.6 5.9 %collective-permute-done.22 = f32[256,256]{1,0:T(8,128)S(1)} collective-permute-done((f32[256,256]{1,0:T(8,128)S(1)}, f32[256,256]{1,0:T(8,128)S(1)}, u32[]{:S(2)}, u32[]{:S(2)}) %collective-permute-start.22) | collective-permute-done | bytes 262176 | tf_op jit(solution)/shard_map/ppermute | solution.py:192
  132.3 4.7 %collective-permute-done.23 = f32[256,256]{1,0:T(8,128)S(1)} collective-permute-done((f32[256,256]{1,0:T(8,128)S(1)}, f32[256,256]{1,0:T(8,128)S(1)}, u32[]{:S(2)}, u32[]{:S(2)}) %collective-permute-start.23) | collective-permute-done | bytes 262176 | tf_op jit(solution)/shard_map/ppermute | solution.py:192
  137.0 2.7 %collective-permute-start.24 = (f32[256,256]{1,0:T(8,128)S(1)}, f32[256,256]{1,0:T(8,128)S(1)}, u32[]{:S(2)}, u32[]{:S(2)}) collective-permute-start(f32[256,256]{1,0:T(8,128)S(1)} %add.47.own_ref), channel_id=1, source_target_pairs={{0,16},{1,17},{2,18},{3,19},{4,20},{5,21},{6,22},{7,23},{8,24},{9,... | collective-permute-start | bytes 786440 | tf_op jit(solution)/shard_map/ppermute | solution.py:192
  140.4 9.2 %collective-permute-done.24.sib_ref = f32[256,256]{1,0:T(8,128)S(1)} collective-permute-done((f32[256,256]{1,0:T(8,128)S(1)}, f32[256,256]{1,0:T(8,128)S(1)}, u32[]{:S(2)}, u32[]{:S(2)}) %collective-permute-start.24) | collective-permute-done | bytes 262176 | tf_op jit(solution)/shard_map/ppermute | solution.py:192
  151.8 5.3 %shard_map.43.w_ref = f32[1024,128]{1,0:T(8,128)} custom-call(s32[1]{0:T(128)} %bitcast.par_ref, f32[256,256]{1,0:T(8,128)} %copy-done.6, f32[256,256]{1,0:T(8,128)} %copy-done.11, f32[256,128]{1,0:T(8,128)} %copy-done.18, f32[256,128]{1,0:T(8,128)} %copy-done.23, f32[256,256]{1,0:T(8,128)} %get-tuple-element.46.refs_0_, ...), custom_call_target="tpu_custom_call" | custom-call | flops 3000000000 | bytes 4000000 | tf_op jit(solution)/shard_map/pallas_call | solution.py:141
  157.2 2.0 %collective-permute-done.30.w_other_ref = f32[1024,128]{1,0:T(8,128)S(1)} collective-permute-done((f32[1024,128]{1,0:T(8,128)}, f32[1024,128]{1,0:T(8,128)S(1)}, u32[]{:S(2)}, u32[]{:S(2)}) %collective-permute-start.30) | collective-permute-done | bytes 524320 | tf_op jit(solution)/shard_map/ppermute | solution.py:192
  160.0 8.2 %shard_map.44 = f32[2048,256]{1,0:T(8,128)} custom-call(s32[1]{0:T(128)} %bitcast.par_ref, f32[2048,256]{1,0:T(8,128)} %b_ref.7, f32[4,2048,256]{2,1,0:T(8,128)} %u_ref.7, f32[1024,128]{1,0:T(8,128)} %shard_map.43.w_ref, f32[1024,128]{1,0:T(8,128)} %copy-done.7), custom_call_target="tpu_custom_call" | custom-call | tf_op jit(solution)/shard_map/pallas_call | solution.py:172
  (137 shorter events, 34.0 us)
Async XLA Ops:
  12.7 18.0 %collective-permute-start.1 = (f32[256,640]{1,0:T(8,128)S(1)}, f32[256,640]{1,0:T(8,128)S(1)}, u32[]{:S(2)}, u32[]{:S(2)}) collective-permute-start(f32[256,640]{1,0:T(8,128)S(1)} %add.37.own_ref), channel_id=1, source_target_pairs={{0,2},{1,3},{2,0},{3,1},{4,6},{5,7},{6,4},{7,5},{8,10},{9,11},{10,... | collective-permute-start | bytes 1966088 | tf_op jit(solution)/shard_map/ppermute | solution.py:192
  30.7 4.6 %collective-permute-start.2 = (f32[256,128]{1,0:T(8,128)S(1)}, f32[256,128]{1,0:T(8,128)S(1)}, u32[]{:S(2)}, u32[]{:S(2)}) collective-permute-start(f32[256,128]{1,0:T(8,128)S(1)} %slice.88), channel_id=1, source_target_pairs={{0,1},{1,0},{2,3},{3,2},{4,5},{5,4},{6,7},{7,6},{8,9},{9,8},{10,11... | collective-permute-start | bytes 393224 | tf_op jit(solution)/shard_map/ppermute | solution.py:192
  31.2 4.0 %collective-permute-start.3 = (f32[256,128]{1,0:T(8,128)S(1)}, f32[256,128]{1,0:T(8,128)S(1)}, u32[]{:S(2)}, u32[]{:S(2)}) collective-permute-start(f32[256,128]{1,0:T(8,128)S(1)} %slice.89), channel_id=1, source_target_pairs={{0,1},{1,0},{2,3},{3,2},{4,5},{5,4},{6,7},{7,6},{8,9},{9,8},{10,11... | collective-permute-start | bytes 393224 | tf_op jit(solution)/shard_map/ppermute | solution.py:192
  44.5 16.5 %collective-permute-start.6 = (f32[168,512]{1,0:T(8,128)S(1)}, f32[168,512]{1,0:T(8,128)S(1)}, u32[]{:S(2)}, u32[]{:S(2)}) collective-permute-start(f32[168,512]{1,0:T(8,128)S(1)} %slice.92), channel_id=1, source_target_pairs={{0,2},{1,3},{2,0},{3,1},{4,6},{5,7},{6,4},{7,5},{8,10},{9,11},{10,... | collective-permute-start | bytes 1032200 | tf_op jit(solution)/shard_map/ppermute | solution.py:192
  46.4 14.7 %collective-permute-start.7 = (f32[88,512]{1,0:T(8,128)S(1)}, f32[88,512]{1,0:T(8,128)S(1)}, u32[]{:S(2)}, u32[]{:S(2)}) collective-permute-start(f32[88,512]{1,0:T(8,128)S(1)} %slice.93), channel_id=1, source_target_pairs={{0,4},{1,5},{2,6},{3,7},{4,0},{5,1},{6,2},{7,3},{8,12},{9,13},{10,... | collective-permute-start | bytes 540680 | tf_op jit(solution)/shard_map/ppermute | solution.py:192
  61.0 3.4 %collective-permute-start.12 = (f32[512,640]{1,0:T(8,128)}, f32[512,640]{1,0:T(8,128)}, u32[]{:S(2)}, u32[]{:S(2)}) collective-permute-start(f32[512,640]{1,0:T(8,128)} %get-tuple-element.41), channel_id=1, source_target_pairs={{0,1},{1,0},{2,3},{3,2},{4,5},{5,4},{6,7},{7,6},{8,9},{9,8},{10,11... | collective-permute-start | bytes 3932168 | tf_op jit(solution)/shard_map/ppermute | solution.py:192
  61.1 10.9 %collective-permute-start.8 = (f32[176,512]{1,0:T(8,128)S(1)}, f32[176,512]{1,0:T(8,128)S(1)}, u32[]{:S(2)}, u32[]{:S(2)}) collective-permute-start(f32[176,512]{1,0:T(8,128)S(1)} %pad_maximum_fusion.2), channel_id=1, source_target_pairs={{0,2},{1,3},{2,0},{3,1},{4,6},{5,7},{6,4},{7,5},{8,10},{9,11},{10,... | collective-permute-start | bytes 1081352 | tf_op jit(solution)/shard_map/ppermute | solution.py:192
  61.8 10.3 %collective-permute-start.9 = (f32[168,512]{1,0:T(8,128)S(1)}, f32[168,512]{1,0:T(8,128)S(1)}, u32[]{:S(2)}, u32[]{:S(2)}) collective-permute-start(f32[168,512]{1,0:T(8,128)S(1)} %slice_add_fusion.2), channel_id=1, source_target_pairs={{0,4},{1,5},{2,6},{3,7},{4,0},{5,1},{6,2},{7,3},{8,12},{9,13},{10,... | collective-permute-start | bytes 1032200 | tf_op jit(solution)/shard_map/ppermute | solution.py:192
  66.0 6.2 %collective-permute-start.13 = (f32[512,128]{1,0:T(8,128)S(1)}, f32[512,128]{1,0:T(8,128)S(1)}, u32[]{:S(2)}, u32[]{:S(2)}) collective-permute-start(f32[512,128]{1,0:T(8,128)S(1)} %slice.124), channel_id=1, source_target_pairs={{0,1},{1,0},{2,3},{3,2},{4,5},{5,4},{6,7},{7,6},{8,9},{9,8},{10,11... | collective-permute-start | bytes 786440 | tf_op jit(solution)/shard_map/ppermute | solution.py:192
  72.1 4.7 %collective-permute-start.11 = (f32[256,128]{1,0:T(8,128)S(1)}, f32[256,128]{1,0:T(8,128)S(1)}, u32[]{:S(2)}, u32[]{:S(2)}) collective-permute-start(f32[256,128]{1,0:T(8,128)S(1)} %fusion.12), channel_id=1, source_target_pairs={{0,1},{1,0},{2,3},{3,2},{4,5},{5,4},{6,7},{7,6},{8,9},{9,8},{10,11... | collective-permute-start | bytes 393224 | tf_op jit(solution)/shard_map/ppermute | solution.py:192
  73.5 3.3 %collective-permute-start.10 = (f32[256,128]{1,0:T(8,128)S(1)}, f32[256,128]{1,0:T(8,128)S(1)}, u32[]{:S(2)}, u32[]{:S(2)}) collective-permute-start(f32[256,128]{1,0:T(8,128)S(1)} %fusion.13), channel_id=1, source_target_pairs={{0,1},{1,0},{2,3},{3,2},{4,5},{5,4},{6,7},{7,6},{8,9},{9,8},{10,11... | collective-permute-start | bytes 393224 | tf_op jit(solution)/shard_map/ppermute | solution.py:192
  83.0 8.0 %collective-permute-start.15 = (f32[256,384]{1,0:T(8,128)}, f32[256,384]{1,0:T(8,128)S(1)}, u32[]{:S(2)}, u32[]{:S(2)}) collective-permute-start(f32[256,384]{1,0:T(8,128)} %get-tuple-element.43), channel_id=1, source_target_pairs={{0,2},{1,5},{2,0},{3,7},{4,6},{5,1},{6,4},{7,3},{8,10},{9,13},{10,... | collective-permute-start | bytes 1179656 | tf_op jit(solution)/shard_map/ppermute | solution.py:192
  92.0 7.8 %collective-permute-start.16 = (f32[256,384]{1,0:T(8,128)S(1)}, f32[256,384]{1,0:T(8,128)S(1)}, u32[]{:S(2)}, u32[]{:S(2)}) collective-permute-start(f32[256,384]{1,0:T(8,128)S(1)} %add.43), channel_id=1, source_target_pairs={{0,4},{1,3},{2,6},{3,1},{4,0},{5,7},{6,2},{7,5},{8,12},{9,11},{10,... | collective-permute-start | bytes 1179656 | tf_op jit(solution)/shard_map/ppermute | solution.py:192
  99.9 9.9 %collective-permute-start.17 = (f32[256,384]{1,0:T(8,128)S(1)}, f32[256,384]{1,0:T(8,128)S(1)}, u32[]{:S(2)}, u32[]{:S(2)}) collective-permute-start(f32[256,384]{1,0:T(8,128)S(1)} %add.44.own_ref), channel_id=1, source_target_pairs={{0,8},{1,9},{2,10},{3,11},{4,12},{5,13},{6,14},{7,15},{8,0},{9,1},... | collective-permute-start | bytes 1179656 | tf_op jit(solution)/shard_map/ppermute | solution.py:192
  102.0 8.7 %collective-permute-start.20 = (f32[256,128]{1,0:T(8,128)S(1)}, f32[256,128]{1,0:T(8,128)S(1)}, u32[]{:S(2)}, u32[]{:S(2)}) collective-permute-start(f32[256,128]{1,0:T(8,128)S(1)} %slice.134.col_ref), channel_id=1, source_target_pairs={{0,1},{1,0},{2,3},{3,2},{4,5},{5,4},{6,7},{7,6},{8,9},{9,8},{10,11... | collective-permute-start | bytes 393224 | tf_op jit(solution)/shard_map/ppermute | solution.py:192
  102.1 8.6 %collective-permute-start.18 = (f32[256,128]{1,0:T(8,128)S(1)}, f32[256,128]{1,0:T(8,128)S(1)}, u32[]{:S(2)}, u32[]{:S(2)}) collective-permute-start(f32[256,128]{1,0:T(8,128)S(1)} %slice.128), channel_id=1, source_target_pairs={{0,1},{1,0},{2,3},{3,2},{4,5},{5,4},{6,7},{7,6},{8,9},{9,8},{10,11... | collective-permute-start | bytes 393224 | tf_op jit(solution)/shard_map/ppermute | solution.py:192
  116.4 6.6 %collective-permute-start.21 = (f32[256,256]{1,0:T(8,128)}, f32[256,256]{1,0:T(8,128)S(1)}, u32[]{:S(2)}, u32[]{:S(2)}) collective-permute-start(f32[256,256]{1,0:T(8,128)} %get-tuple-element.45), channel_id=1, source_target_pairs={{0,2},{1,5},{2,0},{3,7},{4,6},{5,1},{6,4},{7,3},{8,10},{9,13},{10,... | collective-permute-start | bytes 786440 | tf_op jit(solution)/shard_map/ppermute | solution.py:192
  124.0 6.4 %collective-permute-start.22 = (f32[256,256]{1,0:T(8,128)S(1)}, f32[256,256]{1,0:T(8,128)S(1)}, u32[]{:S(2)}, u32[]{:S(2)}) collective-permute-start(f32[256,256]{1,0:T(8,128)S(1)} %add.45), channel_id=1, source_target_pairs={{0,4},{1,9},{2,6},{3,11},{4,0},{5,13},{6,2},{7,15},{8,12},{9,1},{1... | collective-permute-start | bytes 786440 | tf_op jit(solution)/shard_map/ppermute | solution.py:192
  130.5 6.4 %collective-permute-start.23 = (f32[256,256]{1,0:T(8,128)S(1)}, f32[256,256]{1,0:T(8,128)S(1)}, u32[]{:S(2)}, u32[]{:S(2)}) collective-permute-start(f32[256,256]{1,0:T(8,128)S(1)} %add.46), channel_id=1, source_target_pairs={{0,8},{1,3},{2,10},{3,1},{4,12},{5,7},{6,14},{7,5},{8,0},{9,11},{1... | collective-permute-start | bytes 786440 | tf_op jit(solution)/shard_map/ppermute | solution.py:192
  132.2 17.6 %collective-permute-start.29 = (f32[256,384]{1,0:T(8,128)S(1)}, f32[256,384]{1,0:T(8,128)S(1)}, u32[]{:S(2)}, u32[]{:S(2)}) collective-permute-start(f32[256,384]{1,0:T(8,128)S(1)} %slice.114), channel_id=1, source_target_pairs={{0,1},{1,0},{2,3},{3,2},{4,5},{5,4},{6,7},{7,6},{8,9},{9,8},{10,11... | collective-permute-start | bytes 1179656 | tf_op jit(solution)/shard_map/ppermute | solution.py:192
  137.0 12.7 %collective-permute-start.24 = (f32[256,256]{1,0:T(8,128)S(1)}, f32[256,256]{1,0:T(8,128)S(1)}, u32[]{:S(2)}, u32[]{:S(2)}) collective-permute-start(f32[256,256]{1,0:T(8,128)S(1)} %add.47.own_ref), channel_id=1, source_target_pairs={{0,16},{1,17},{2,18},{3,19},{4,20},{5,21},{6,22},{7,23},{8,24},{9,... | collective-permute-start | bytes 786440 | tf_op jit(solution)/shard_map/ppermute | solution.py:192
  139.7 10.1 %collective-permute-start.28 = (f32[256,256]{1,0:T(8,128)S(1)}, f32[256,256]{1,0:T(8,128)S(1)}, u32[]{:S(2)}, u32[]{:S(2)}) collective-permute-start(f32[256,256]{1,0:T(8,128)S(1)} %slice.113), channel_id=1, source_target_pairs={{0,1},{1,0},{2,3},{3,2},{4,5},{5,4},{6,7},{7,6},{8,9},{9,8},{10,11... | collective-permute-start | bytes 786440 | tf_op jit(solution)/shard_map/ppermute | solution.py:192
  139.8 10.0 %collective-permute-start.27 = (f32[256,128]{1,0:T(8,128)S(1)}, f32[256,128]{1,0:T(8,128)S(1)}, u32[]{:S(2)}, u32[]{:S(2)}) collective-permute-start(f32[256,128]{1,0:T(8,128)S(1)} %slice.112), channel_id=1, source_target_pairs={{0,1},{1,0},{2,3},{3,2},{4,5},{5,4},{6,7},{7,6},{8,9},{9,8},{10,11... | collective-permute-start | bytes 393224 | tf_op jit(solution)/shard_map/ppermute | solution.py:192
  140.3 9.5 %collective-permute-start.25 = (f32[256,128]{1,0:T(8,128)S(1)}, f32[256,128]{1,0:T(8,128)S(1)}, u32[]{:S(2)}, u32[]{:S(2)}) collective-permute-start(f32[256,128]{1,0:T(8,128)S(1)} %slice.135), channel_id=1, source_target_pairs={{0,1},{1,0},{2,3},{3,2},{4,5},{5,4},{6,7},{7,6},{8,9},{9,8},{10,11... | collective-permute-start | bytes 393224 | tf_op jit(solution)/shard_map/ppermute | solution.py:192
  (34 other events, 147.4 us)

commit v3 on v2

--- a/solution.py
+++ b/solution.py
@@ -111,12 +111,16 @@
     return lax.while_loop(going, sweep, state)[3]
 
 
-def solve_kernel(par_ref, own_ref, sib_ref, own_other_ref, sib_other_ref, row_ref, col_ref, col_other_ref, z_ref, next_ref):
+def solve_kernel(par_ref, own_ref, sib_ref, own_other_ref, sib_other_ref, row_ref, col_ref, col_other_ref, z_ref, *next_refs):
     parity = par_ref[0]
     answer = solve_values(parity, own_ref, sib_ref, own_other_ref, sib_other_ref)
     z_ref[...] = answer
     column = joined(parity, col_ref[...], col_other_ref[...])
-    next_ref[...] = row_ref[:, : answer.shape[1]] - mm(column, answer)
+    following = row_ref[:, : answer.shape[1]] - mm(column, answer)
+    start = 0
+    for next_ref in next_refs:
+        next_ref[...] = following[start : start + next_ref.shape[0]]
+        start += next_ref.shape[0]
 
 
 def top_kernel(count, par_ref, own_ref, sib_ref, own_other_ref, sib_other_ref, *refs):
@@ -216,7 +220,7 @@
             low, low_far = gram(later, v, b, u, 0, levels - 2, tile)
         if sibling == 2:
             cut = rank * 2 // 3 // 8 * 8
-            early, late = own[:cut], own[cut:]
+            early, late = own if isinstance(own, list) else (own[:cut], own[cut:])
             early_pair, late_far = swap(early, 1, 1), swap(late, 2, 2)
             if k == levels - 2:
                 early_pair, late_far, low_far = lax.optimization_barrier((early_pair, late_far, low_far))
@@ -254,13 +258,17 @@
             cols_other = swap(cols, 0, 0)
             last = slice((len(near) - 1) * rank, len(near) * rank)
             shape = jax.ShapeDtypeStruct((rank, width), F32)
-            z, following = small_call(
-                solve_kernel, (shape, shape), parity, own, sib, own_other, sib_other,
+            pieces = [rank]
+            if sibling == 1:
+                cut = rank * 2 // 3 // 8 * 8
+                pieces = [cut, rank - cut]
+            z, *following = small_call(
+                solve_kernel, (shape, *[jax.ShapeDtypeStruct((p, width), F32) for p in pieces]), parity, own, sib, own_other, sib_other,
                 rows[k - 1][:, :width], cols[last], cols_other[last],
             )
             answers[k] = z
             answers_other[k] = swap(z[:, half:], 0, 0)
-            rows[k - 1] = following
+            rows[k - 1] = following if len(pieces) > 1 else following[0]
             if len(near) > 1:
                 before = slice(0, (k - 1) * rank)
                 column = joined(parity[0], cols[before], cols_other[before])

time: 169 us -> 169 us (level)
  waiting for transfers between devices: 67.7 us -> 71.2 us
  starting transfers between devices: 21.2 us -> 19.1 us
  local copies, waits for them, and re-layouts: 8.6 us -> 6.62 us
    ppermute x31, waiting for transfers between devices: 67.7 us -> 71.2 us  [swap(): return lax.ppermute(block, AXES, route)]
    ppermute x31, starting transfers between devices: 21.2 us -> 19.1 us  [swap(): return lax.ppermute(block, AXES, route)]
    slice x2 -> x0, local copies, waits for them, and re-layouts: 1.94 us -> none  [local(): early, late = (own[:cut], own[cut:])]
    unnamed x54 -> x60, local copies, waits for them, and re-layouts: 4.02 us -> 3.98 us
  transfers between devices with their start and end apart: 31 -> 31, of which waited for: 16 -> 16; matrix products, arithmetic and copies ran while one was open for 5% -> 6% of each run, Pallas kernels for 13% -> 13%
where the time goes in v3:
time: 169 us; the launch traced here: 168 us
  waiting for transfers between devices  71.2 us (42%)
  Pallas kernels  60.7 us (36%)
  starting transfers between devices  19.1 us (11%)
  other arithmetic  8.93 us (5%)
  local copies, waits for them, and re-layouts  6.62 us (4%)
    ppermute x31, waiting for transfers between devices, swap(): return lax.ppermute(block, AXES, route)  71.2 us
    pallas_call x3, Pallas kernels, gram(): pl.pallas_call(gram_kernel, grid=(rows // tile,), out_shape=(shape, shape...  31.3 us
    pallas_call x4, Pallas kernels, small_call(): pl.pallas_call(kernel, out_shape=shapes, in_specs=[pl.BlockSpec(memory_sp...  21.2 us
    ppermute x31, starting transfers between devices, swap(): return lax.ppermute(block, AXES, route)  19.1 us
    pallas_call x1, Pallas kernels, apply(): pl.pallas_call(apply_kernel, grid=(rows // tile,), out_shape=jax.ShapeDty...  8.16 us
    unnamed x60, local copies, waits for them, and re-layouts  3.98 us
  transfers between devices with their start and end apart: 31, of which 16 were waited for; matrix products, arithmetic and copies ran while one was open for 6% of the time, Pallas kernels for 13%

profile of v3, /device:TPU:0, one launch (start us, length us, event | category | flops | bytes accessed | tf_op | source)
XLA Modules:
  0.0 168.1 jit_solution(9238395134196543432)
XLA Ops:
  0.0 9.1 %shard_map.37 = (f32[256,640]{1,0:T(8,128)}, f32[256,640]{1,0:T(8,128)}) custom-call(s32[1]{0:T(128)} %bitcast.par_ref, f32[4,2048,256]{2,1,0:T(8,128)} %v_ref.5, f32[2048,256]{1,0:T(8,128)} %b_ref.7, f32[4,2048,256]{2,1,0:T(8,128)} %u_ref.7), custom_call_target="tpu_custom_call" | custom-call | flops 4026531840 | bytes 13893632 | tf_op jit(solution)/shard_map/pallas_call | solution.py:70
  9.6 1.9 %collective-permute-done = f32[256,640]{1,0:T(8,128)S(1)} collective-permute-done((f32[256,640]{1,0:T(8,128)}, f32[256,640]{1,0:T(8,128)S(1)}, u32[]{:S(2)}, u32[]{:S(2)}) %collective-permute-start) | collective-permute-done | bytes 655392 | tf_op jit(solution)/shard_map/ppermute | solution.py:196
  12.7 2.9 %collective-permute-start.1 = (f32[256,640]{1,0:T(8,128)S(1)}, f32[256,640]{1,0:T(8,128)S(1)}, u32[]{:S(2)}, u32[]{:S(2)}) collective-permute-start(f32[256,640]{1,0:T(8,128)S(1)} %add.37.own_ref), channel_id=1, source_target_pairs={{0,2},{1,3},{2,0},{3,1},{4,6},{5,7},{6,4},{7,5},{8,10},{9,11},{10,... | collective-permute-start | bytes 1966088 | tf_op jit(solution)/shard_map/ppermute | solution.py:196
  15.6 9.1 %shard_map.38 = (f32[256,640]{1,0:T(8,128)}, f32[256,640]{1,0:T(8,128)}) custom-call(s32[1]{0:T(128)} %bitcast.par_ref, f32[4,2048,256]{2,1,0:T(8,128)} %v_ref.5, f32[2048,256]{1,0:T(8,128)} %b_ref.7, f32[4,2048,256]{2,1,0:T(8,128)} %u_ref.7), custom_call_target="tpu_custom_call" | custom-call | flops 4026531840 | bytes 13893632 | tf_op jit(solution)/shard_map/pallas_call | solution.py:70
  24.7 5.9 %collective-permute-done.1.sib_ref = f32[256,640]{1,0:T(8,128)S(1)} collective-permute-done((f32[256,640]{1,0:T(8,128)S(1)}, f32[256,640]{1,0:T(8,128)S(1)}, u32[]{:S(2)}, u32[]{:S(2)}) %collective-permute-start.1) | collective-permute-done | bytes 655392 | tf_op jit(solution)/shard_map/ppermute | solution.py:196
  31.3 1.6 collective-permute-done.4
  36.6 6.0 %shard_map.39 = (f32[256,512]{1,0:T(8,128)}, f32[168,512]{1,0:T(8,128)}, f32[88,512]{1,0:T(8,128)}) custom-call(s32[1]{0:T(128)} %bitcast.par_ref, f32[256,640]{1,0:T(8,128)} %copy-done.3, f32[256,640]{1,0:T(8,128)} %copy-done.16, f32[256,128]{1,0:T(8,128)} %copy-done.21, f32[256,128]{1,0:T(8,128)} %copy-done.23, f32[256,512]{1,0:T(8,128)} %slice.107.row_ref, ...), custom_call_target="tpu_custom_call" | custom-call | flops 3000000000 | bytes 4000000 | tf_op jit(solution)/shard_map/pallas_call | solution.py:145
  42.6 1.7 %collective-permute-start.6 = (f32[168,512]{1,0:T(8,128)}, f32[168,512]{1,0:T(8,128)S(1)}, u32[]{:S(2)}, u32[]{:S(2)}) collective-permute-start(f32[168,512]{1,0:T(8,128)} %get-tuple-element.38), channel_id=1, source_target_pairs={{0,2},{1,3},{2,0},{3,1},{4,6},{5,7},{6,4},{7,5},{8,10},{9,11},{10,... | collective-permute-start | bytes 1032200 | tf_op jit(solution)/shard_map/ppermute | solution.py:196
  45.9 13.1 %shard_map.40 = (f32[512,640]{1,0:T(8,128)}, f32[512,640]{1,0:T(8,128)}) custom-call(s32[1]{0:T(128)} %bitcast.par_ref, f32[4,2048,256]{2,1,0:T(8,128)} %v_ref.5, f32[2048,256]{1,0:T(8,128)} %b_ref.7, f32[4,2048,256]{2,1,0:T(8,128)} %u_ref.7), custom_call_target="tpu_custom_call" | custom-call | flops 8053063680 | bytes 17301504 | tf_op jit(solution)/shard_map/pallas_call | solution.py:70
  62.7 8.3 %collective-permute-done.8 = f32[176,512]{1,0:T(8,128)} collective-permute-done((f32[176,512]{1,0:T(8,128)}, f32[176,512]{1,0:T(8,128)}, u32[]{:S(2)}, u32[]{:S(2)}) %collective-permute-start.8) | collective-permute-done | bytes 360480 | tf_op jit(solution)/shard_map/ppermute | solution.py:196
  77.4 5.5 %shard_map.41 = (f32[256,384]{1,0:T(8,128)}, f32[256,384]{1,0:T(8,128)}) custom-call(s32[1]{0:T(128)} %bitcast.par_ref, f32[256,512]{1,0:T(8,128)} %pad_maximum_fusion.own_ref, f32[256,512]{1,0:T(8,128)} %pad_maximum_fusion.1.sib_ref, f32[256,128]{1,0:T(8,128)} %copy-done.25, f32[256,128]{1,0:T(8,128)} %copy-done.19, f32[256,384]{1,0:T(8,128)} %slice.117.row_ref, ...), custom_call_target="tpu_custom_call" | custom-call | flops 3000000000 | bytes 4000000 | tf_op jit(solution)/shard_map/pallas_call | solution.py:145
  83.5 7.5 %collective-permute-done.15 = f32[256,384]{1,0:T(8,128)S(1)} collective-permute-done((f32[256,384]{1,0:T(8,128)}, f32[256,384]{1,0:T(8,128)S(1)}, u32[]{:S(2)}, u32[]{:S(2)}) %collective-permute-start.15) | collective-permute-done | bytes 393248 | tf_op jit(solution)/shard_map/ppermute | solution.py:196
  92.6 7.3 %collective-permute-done.16 = f32[256,384]{1,0:T(8,128)S(1)} collective-permute-done((f32[256,384]{1,0:T(8,128)S(1)}, f32[256,384]{1,0:T(8,128)S(1)}, u32[]{:S(2)}, u32[]{:S(2)}) %collective-permute-start.16) | collective-permute-done | bytes 393248 | tf_op jit(solution)/shard_map/ppermute | solution.py:196
  102.6 7.2 %collective-permute-done.17.sib_ref = f32[256,384]{1,0:T(8,128)S(1)} collective-permute-done((f32[256,384]{1,0:T(8,128)S(1)}, f32[256,384]{1,0:T(8,128)S(1)}, u32[]{:S(2)}, u32[]{:S(2)}) %collective-permute-start.17) | collective-permute-done | bytes 393248 | tf_op jit(solution)/shard_map/ppermute | solution.py:196
  112.0 4.4 %shard_map.42 = (f32[256,256]{1,0:T(8,128)}, f32[256,256]{1,0:T(8,128)}) custom-call(s32[1]{0:T(128)} %bitcast.par_ref, f32[256,384]{1,0:T(8,128)} %copy-done.7, f32[256,384]{1,0:T(8,128)} %copy-done.15, f32[256,128]{1,0:T(8,128)} %copy-done.27, f32[256,128]{1,0:T(8,128)} %copy-done.29, f32[256,256]{1,0:T(8,128)} %slice.125.row_ref, f32[256,128]{1,0:T(8,128)} %copy-done.11, ...), custom_call_target="tpu_custom_call" | custom-call | flops 3000000000 | bytes 4000000 | tf_op jit(solution)/shard_map/pallas_call | solution.py:145
  116.9 6.0 %collective-permute-done.21 = f32[256,256]{1,0:T(8,128)S(1)} collective-permute-done((f32[256,256]{1,0:T(8,128)}, f32[256,256]{1,0:T(8,128)S(1)}, u32[]{:S(2)}, u32[]{:S(2)}) %collective-permute-start.21) | collective-permute-done | bytes 262176 | tf_op jit(solution)/shard_map/ppermute | solution.py:196
  124.5 5.9 %collective-permute-done.22 = f32[256,256]{1,0:T(8,128)S(1)} collective-permute-done((f32[256,256]{1,0:T(8,128)S(1)}, f32[256,256]{1,0:T(8,128)S(1)}, u32[]{:S(2)}, u32[]{:S(2)}) %collective-permute-start.22) | collective-permute-done | bytes 262176 | tf_op jit(solution)/shard_map/ppermute | solution.py:196
  130.4 1.6 collective-permute-start.23
  132.2 4.7 %collective-permute-done.23 = f32[256,256]{1,0:T(8,128)S(1)} collective-permute-done((f32[256,256]{1,0:T(8,128)S(1)}, f32[256,256]{1,0:T(8,128)S(1)}, u32[]{:S(2)}, u32[]{:S(2)}) %collective-permute-start.23) | collective-permute-done | bytes 262176 | tf_op jit(solution)/shard_map/ppermute | solution.py:196
  136.9 2.6 %collective-permute-start.24 = (f32[256,256]{1,0:T(8,128)S(1)}, f32[256,256]{1,0:T(8,128)S(1)}, u32[]{:S(2)}, u32[]{:S(2)}) collective-permute-start(f32[256,256]{1,0:T(8,128)S(1)} %add.47.own_ref), channel_id=1, source_target_pairs={{0,16},{1,17},{2,18},{3,19},{4,20},{5,21},{6,22},{7,23},{8,24},{9,... | collective-permute-start | bytes 786440 | tf_op jit(solution)/shard_map/ppermute | solution.py:196
  140.3 9.2 %collective-permute-done.24.sib_ref = f32[256,256]{1,0:T(8,128)S(1)} collective-permute-done((f32[256,256]{1,0:T(8,128)S(1)}, f32[256,256]{1,0:T(8,128)S(1)}, u32[]{:S(2)}, u32[]{:S(2)}) %collective-permute-start.24) | collective-permute-done | bytes 262176 | tf_op jit(solution)/shard_map/ppermute | solution.py:196
  151.7 5.3 %shard_map.43.w_ref = f32[1024,128]{1,0:T(8,128)} custom-call(s32[1]{0:T(128)} %bitcast.par_ref, f32[256,256]{1,0:T(8,128)} %copy-done.8, f32[256,256]{1,0:T(8,128)} %copy-done.14, f32[256,128]{1,0:T(8,128)} %copy-done.22, f32[256,128]{1,0:T(8,128)} %copy-done.26, f32[256,256]{1,0:T(8,128)} %get-tuple-element.50.refs_0_, ...), custom_call_target="tpu_custom_call" | custom-call | flops 3000000000 | bytes 4000000 | tf_op jit(solution)/shard_map/pallas_call | solution.py:145
  157.2 2.0 %collective-permute-done.30.w_other_ref = f32[1024,128]{1,0:T(8,128)S(1)} collective-permute-done((f32[1024,128]{1,0:T(8,128)}, f32[1024,128]{1,0:T(8,128)S(1)}, u32[]{:S(2)}, u32[]{:S(2)}) %collective-permute-start.30) | collective-permute-done | bytes 524320 | tf_op jit(solution)/shard_map/ppermute | solution.py:196
  159.9 8.2 %shard_map.44 = f32[2048,256]{1,0:T(8,128)} custom-call(s32[1]{0:T(128)} %bitcast.par_ref, f32[2048,256]{1,0:T(8,128)} %b_ref.7, f32[4,2048,256]{2,1,0:T(8,128)} %u_ref.7, f32[1024,128]{1,0:T(8,128)} %shard_map.43.w_ref, f32[1024,128]{1,0:T(8,128)} %copy-done.9), custom_call_target="tpu_custom_call" | custom-call | tf_op jit(solution)/shard_map/pallas_call | solution.py:176
  (141 shorter events, 30.4 us)
Async XLA Ops:
  12.7 18.0 %collective-permute-start.1 = (f32[256,640]{1,0:T(8,128)S(1)}, f32[256,640]{1,0:T(8,128)S(1)}, u32[]{:S(2)}, u32[]{:S(2)}) collective-permute-start(f32[256,640]{1,0:T(8,128)S(1)} %add.37.own_ref), channel_id=1, source_target_pairs={{0,2},{1,3},{2,0},{3,1},{4,6},{5,7},{6,4},{7,5},{8,10},{9,11},{10,... | collective-permute-start | bytes 1966088 | tf_op jit(solution)/shard_map/ppermute | solution.py:196
  30.7 4.6 %collective-permute-start.2 = (f32[256,128]{1,0:T(8,128)S(1)}, f32[256,128]{1,0:T(8,128)S(1)}, u32[]{:S(2)}, u32[]{:S(2)}) collective-permute-start(f32[256,128]{1,0:T(8,128)S(1)} %slice.82), channel_id=1, source_target_pairs={{0,1},{1,0},{2,3},{3,2},{4,5},{5,4},{6,7},{7,6},{8,9},{9,8},{10,11... | collective-permute-start | bytes 393224 | tf_op jit(solution)/shard_map/ppermute | solution.py:196
  31.2 4.0 %collective-permute-start.3 = (f32[256,128]{1,0:T(8,128)S(1)}, f32[256,128]{1,0:T(8,128)S(1)}, u32[]{:S(2)}, u32[]{:S(2)}) collective-permute-start(f32[256,128]{1,0:T(8,128)S(1)} %slice.83), channel_id=1, source_target_pairs={{0,1},{1,0},{2,3},{3,2},{4,5},{5,4},{6,7},{7,6},{8,9},{9,8},{10,11... | collective-permute-start | bytes 393224 | tf_op jit(solution)/shard_map/ppermute | solution.py:196
  42.6 16.4 %collective-permute-start.6 = (f32[168,512]{1,0:T(8,128)}, f32[168,512]{1,0:T(8,128)S(1)}, u32[]{:S(2)}, u32[]{:S(2)}) collective-permute-start(f32[168,512]{1,0:T(8,128)} %get-tuple-element.38), channel_id=1, source_target_pairs={{0,2},{1,3},{2,0},{3,1},{4,6},{5,7},{6,4},{7,5},{8,10},{9,11},{10,... | collective-permute-start | bytes 1032200 | tf_op jit(solution)/shard_map/ppermute | solution.py:196
  44.3 14.7 %collective-permute-start.7 = (f32[88,512]{1,0:T(8,128)}, f32[88,512]{1,0:T(8,128)S(1)}, u32[]{:S(2)}, u32[]{:S(2)}) collective-permute-start(f32[88,512]{1,0:T(8,128)} %get-tuple-element.39), channel_id=1, source_target_pairs={{0,4},{1,5},{2,6},{3,7},{4,0},{5,1},{6,2},{7,3},{8,12},{9,13},{10,... | collective-permute-start | bytes 540680 | tf_op jit(solution)/shard_map/ppermute | solution.py:196
  59.0 3.3 %collective-permute-start.12 = (f32[512,640]{1,0:T(8,128)}, f32[512,640]{1,0:T(8,128)S(1)}, u32[]{:S(2)}, u32[]{:S(2)}) collective-permute-start(f32[512,640]{1,0:T(8,128)} %get-tuple-element.45), channel_id=1, source_target_pairs={{0,1},{1,0},{2,3},{3,2},{4,5},{5,4},{6,7},{7,6},{8,9},{9,8},{10,11... | collective-permute-start | bytes 3932168 | tf_op jit(solution)/shard_map/ppermute | solution.py:196
  59.8 11.1 %collective-permute-start.8 = (f32[176,512]{1,0:T(8,128)}, f32[176,512]{1,0:T(8,128)}, u32[]{:S(2)}, u32[]{:S(2)}) collective-permute-start(f32[176,512]{1,0:T(8,128)} %pad_maximum_fusion.2), channel_id=1, source_target_pairs={{0,2},{1,3},{2,0},{3,1},{4,6},{5,7},{6,4},{7,5},{8,10},{9,11},{10,... | collective-permute-start | bytes 1081352 | tf_op jit(solution)/shard_map/ppermute | solution.py:196
  60.4 11.6 %collective-permute-start.9 = (f32[168,512]{1,0:T(8,128)S(1)}, f32[168,512]{1,0:T(8,128)S(1)}, u32[]{:S(2)}, u32[]{:S(2)}) collective-permute-start(f32[168,512]{1,0:T(8,128)S(1)} %add.39), channel_id=1, source_target_pairs={{0,4},{1,5},{2,6},{3,7},{4,0},{5,1},{6,2},{7,3},{8,12},{9,13},{10,... | collective-permute-start | bytes 1032200 | tf_op jit(solution)/shard_map/ppermute | solution.py:196
  62.5 9.7 %collective-permute-start.13 = (f32[512,128]{1,0:T(8,128)S(1)}, f32[512,128]{1,0:T(8,128)S(1)}, u32[]{:S(2)}, u32[]{:S(2)}) collective-permute-start(f32[512,128]{1,0:T(8,128)S(1)} %slice.116), channel_id=1, source_target_pairs={{0,1},{1,0},{2,3},{3,2},{4,5},{5,4},{6,7},{7,6},{8,9},{9,8},{10,11... | collective-permute-start | bytes 786440 | tf_op jit(solution)/shard_map/ppermute | solution.py:196
  72.1 4.7 %collective-permute-start.11 = (f32[256,128]{1,0:T(8,128)S(1)}, f32[256,128]{1,0:T(8,128)S(1)}, u32[]{:S(2)}, u32[]{:S(2)}) collective-permute-start(f32[256,128]{1,0:T(8,128)S(1)} %fusion.12), channel_id=1, source_target_pairs={{0,1},{1,0},{2,3},{3,2},{4,5},{5,4},{6,7},{7,6},{8,9},{9,8},{10,11... | collective-permute-start | bytes 393224 | tf_op jit(solution)/shard_map/ppermute | solution.py:196
  73.4 3.3 %collective-permute-start.10 = (f32[256,128]{1,0:T(8,128)S(1)}, f32[256,128]{1,0:T(8,128)S(1)}, u32[]{:S(2)}, u32[]{:S(2)}) collective-permute-start(f32[256,128]{1,0:T(8,128)S(1)} %fusion.13), channel_id=1, source_target_pairs={{0,1},{1,0},{2,3},{3,2},{4,5},{5,4},{6,7},{7,6},{8,9},{9,8},{10,11... | collective-permute-start | bytes 393224 | tf_op jit(solution)/shard_map/ppermute | solution.py:196
  83.0 8.0 %collective-permute-start.15 = (f32[256,384]{1,0:T(8,128)}, f32[256,384]{1,0:T(8,128)S(1)}, u32[]{:S(2)}, u32[]{:S(2)}) collective-permute-start(f32[256,384]{1,0:T(8,128)} %get-tuple-element.47), channel_id=1, source_target_pairs={{0,2},{1,5},{2,0},{3,7},{4,6},{5,1},{6,4},{7,3},{8,10},{9,13},{10,... | collective-permute-start | bytes 1179656 | tf_op jit(solution)/shard_map/ppermute | solution.py:196
  92.0 7.8 %collective-permute-start.16 = (f32[256,384]{1,0:T(8,128)S(1)}, f32[256,384]{1,0:T(8,128)S(1)}, u32[]{:S(2)}, u32[]{:S(2)}) collective-permute-start(f32[256,384]{1,0:T(8,128)S(1)} %add.43), channel_id=1, source_target_pairs={{0,4},{1,3},{2,6},{3,1},{4,0},{5,7},{6,2},{7,5},{8,12},{9,11},{10,... | collective-permute-start | bytes 1179656 | tf_op jit(solution)/shard_map/ppermute | solution.py:196
  99.9 9.9 %collective-permute-start.17 = (f32[256,384]{1,0:T(8,128)S(1)}, f32[256,384]{1,0:T(8,128)S(1)}, u32[]{:S(2)}, u32[]{:S(2)}) collective-permute-start(f32[256,384]{1,0:T(8,128)S(1)} %add.44.own_ref), channel_id=1, source_target_pairs={{0,8},{1,9},{2,10},{3,11},{4,12},{5,13},{6,14},{7,15},{8,0},{9,1},... | collective-permute-start | bytes 1179656 | tf_op jit(solution)/shard_map/ppermute | solution.py:196
  101.9 8.7 %collective-permute-start.20 = (f32[256,128]{1,0:T(8,128)S(1)}, f32[256,128]{1,0:T(8,128)S(1)}, u32[]{:S(2)}, u32[]{:S(2)}) collective-permute-start(f32[256,128]{1,0:T(8,128)S(1)} %slice.126.col_ref), channel_id=1, source_target_pairs={{0,1},{1,0},{2,3},{3,2},{4,5},{5,4},{6,7},{7,6},{8,9},{9,8},{10,11... | collective-permute-start | bytes 393224 | tf_op jit(solution)/shard_map/ppermute | solution.py:196
  102.0 8.6 %collective-permute-start.18 = (f32[256,128]{1,0:T(8,128)S(1)}, f32[256,128]{1,0:T(8,128)S(1)}, u32[]{:S(2)}, u32[]{:S(2)}) collective-permute-start(f32[256,128]{1,0:T(8,128)S(1)} %slice.120), channel_id=1, source_target_pairs={{0,1},{1,0},{2,3},{3,2},{4,5},{5,4},{6,7},{7,6},{8,9},{9,8},{10,11... | collective-permute-start | bytes 393224 | tf_op jit(solution)/shard_map/ppermute | solution.py:196
  116.4 6.6 %collective-permute-start.21 = (f32[256,256]{1,0:T(8,128)}, f32[256,256]{1,0:T(8,128)S(1)}, u32[]{:S(2)}, u32[]{:S(2)}) collective-permute-start(f32[256,256]{1,0:T(8,128)} %get-tuple-element.49), channel_id=1, source_target_pairs={{0,2},{1,5},{2,0},{3,7},{4,6},{5,1},{6,4},{7,3},{8,10},{9,13},{10,... | collective-permute-start | bytes 786440 | tf_op jit(solution)/shard_map/ppermute | solution.py:196
  124.0 6.4 %collective-permute-start.22 = (f32[256,256]{1,0:T(8,128)S(1)}, f32[256,256]{1,0:T(8,128)S(1)}, u32[]{:S(2)}, u32[]{:S(2)}) collective-permute-start(f32[256,256]{1,0:T(8,128)S(1)} %add.45), channel_id=1, source_target_pairs={{0,4},{1,9},{2,6},{3,11},{4,0},{5,13},{6,2},{7,15},{8,12},{9,1},{1... | collective-permute-start | bytes 786440 | tf_op jit(solution)/shard_map/ppermute | solution.py:196
  130.4 6.4 %collective-permute-start.23 = (f32[256,256]{1,0:T(8,128)S(1)}, f32[256,256]{1,0:T(8,128)S(1)}, u32[]{:S(2)}, u32[]{:S(2)}) collective-permute-start(f32[256,256]{1,0:T(8,128)S(1)} %add.46), channel_id=1, source_target_pairs={{0,8},{1,3},{2,10},{3,1},{4,12},{5,7},{6,14},{7,5},{8,0},{9,11},{1... | collective-permute-start | bytes 786440 | tf_op jit(solution)/shard_map/ppermute | solution.py:196
  132.1 17.6 %collective-permute-start.29 = (f32[256,384]{1,0:T(8,128)S(1)}, f32[256,384]{1,0:T(8,128)S(1)}, u32[]{:S(2)}, u32[]{:S(2)}) collective-permute-start(f32[256,384]{1,0:T(8,128)S(1)} %slice.106), channel_id=1, source_target_pairs={{0,1},{1,0},{2,3},{3,2},{4,5},{5,4},{6,7},{7,6},{8,9},{9,8},{10,11... | collective-permute-start | bytes 1179656 | tf_op jit(solution)/shard_map/ppermute | solution.py:196
  136.9 12.7 %collective-permute-start.24 = (f32[256,256]{1,0:T(8,128)S(1)}, f32[256,256]{1,0:T(8,128)S(1)}, u32[]{:S(2)}, u32[]{:S(2)}) collective-permute-start(f32[256,256]{1,0:T(8,128)S(1)} %add.47.own_ref), channel_id=1, source_target_pairs={{0,16},{1,17},{2,18},{3,19},{4,20},{5,21},{6,22},{7,23},{8,24},{9,... | collective-permute-start | bytes 786440 | tf_op jit(solution)/shard_map/ppermute | solution.py:196
  139.6 10.1 %collective-permute-start.28 = (f32[256,256]{1,0:T(8,128)S(1)}, f32[256,256]{1,0:T(8,128)S(1)}, u32[]{:S(2)}, u32[]{:S(2)}) collective-permute-start(f32[256,256]{1,0:T(8,128)S(1)} %slice.105), channel_id=1, source_target_pairs={{0,1},{1,0},{2,3},{3,2},{4,5},{5,4},{6,7},{7,6},{8,9},{9,8},{10,11... | collective-permute-start | bytes 786440 | tf_op jit(solution)/shard_map/ppermute | solution.py:196
  139.7 10.0 %collective-permute-start.27 = (f32[256,128]{1,0:T(8,128)S(1)}, f32[256,128]{1,0:T(8,128)S(1)}, u32[]{:S(2)}, u32[]{:S(2)}) collective-permute-start(f32[256,128]{1,0:T(8,128)S(1)} %slice.104), channel_id=1, source_target_pairs={{0,1},{1,0},{2,3},{3,2},{4,5},{5,4},{6,7},{7,6},{8,9},{9,8},{10,11... | collective-permute-start | bytes 393224 | tf_op jit(solution)/shard_map/ppermute | solution.py:196
  140.3 9.5 %collective-permute-start.25 = (f32[256,128]{1,0:T(8,128)S(1)}, f32[256,128]{1,0:T(8,128)S(1)}, u32[]{:S(2)}, u32[]{:S(2)}) collective-permute-start(f32[256,128]{1,0:T(8,128)S(1)} %slice.127), channel_id=1, source_target_pairs={{0,1},{1,0},{2,3},{3,2},{4,5},{5,4},{6,7},{7,6},{8,9},{9,8},{10,11... | collective-permute-start | bytes 393224 | tf_op jit(solution)/shard_map/ppermute | solution.py:196
  (37 other events, 177.8 us)

commit v4 on v3

--- a/solution.py
+++ b/solution.py
@@ -153,19 +153,18 @@
 
 
 def apply_kernel(par_ref, b_ref, u_ref, w_ref, w_other_ref, out_ref, high, low):
-    levels, _, rank = u_ref.shape
+    levels = u_ref.shape[0]
 
     @pl.when(pl.program_id(0) == 0)
     def _():
         high[...], low[...] = split(joined(par_ref[0], w_ref[...], w_other_ref[...]))
 
-    total = b_ref[...]
-    for k in range(levels):
-        u_high, u_low = split(u_ref[k])
-        rows = pl.ds(k * rank, rank)
-        total = total - (
-            dot(u_high, high[rows, :]) + (dot(u_high, low[rows, :]) + dot(u_low, high[rows, :]))
-        )
+    parts = [split(u_ref[k]) for k in range(levels)]
+    u_high = jnp.concatenate([part[0] for part in parts], axis=1)
+    u_low = jnp.concatenate([part[1] for part in parts], axis=1)
+    total = b_ref[...] - (
+        dot(u_high, high[...]) + (dot(u_high, low[...]) + dot(u_low, high[...]))
+    )
     out_ref[...] = total
 
 

time: 169 us -> 169 us (level)
  no operation moved by 1% of the time
where the time goes in v4:
time: 169 us; the launch traced here: 168 us
  waiting for transfers between devices  72.3 us (43%)
  Pallas kernels  60.7 us (36%)
  starting transfers between devices  18 us (11%)
  other arithmetic  8.93 us (5%)
  local copies, waits for them, and re-layouts  6.62 us (4%)
    ppermute x31, waiting for transfers between devices, swap(): return lax.ppermute(block, AXES, route)  72.3 us
    pallas_call x3, Pallas kernels, gram(): pl.pallas_call(gram_kernel, grid=(rows // tile,), out_shape=(shape, shape...  31.3 us
    pallas_call x4, Pallas kernels, small_call(): pl.pallas_call(kernel, out_shape=shapes, in_specs=[pl.BlockSpec(memory_sp...  21.2 us
    ppermute x31, starting transfers between devices, swap(): return lax.ppermute(block, AXES, route)  18 us
    pallas_call x1, Pallas kernels, apply(): pl.pallas_call(apply_kernel, grid=(rows // tile,), out_shape=jax.ShapeDty...  8.14 us
    unnamed x60, local copies, waits for them, and re-layouts  3.98 us
  transfers between devices with their start and end apart: 31, of which 16 were waited for; matrix products, arithmetic and copies ran while one was open for 6% of the time, Pallas kernels for 13%

profile of v4, /device:TPU:0, one launch (start us, length us, event | category | flops | bytes accessed | tf_op | source)
XLA Modules:
  0.0 168.1 jit_solution(11292021977008620800)
XLA Ops:
  0.0 9.1 %shard_map.37 = (f32[256,640]{1,0:T(8,128)}, f32[256,640]{1,0:T(8,128)}) custom-call(s32[1]{0:T(128)} %bitcast.par_ref, f32[4,2048,256]{2,1,0:T(8,128)} %v_ref.5, f32[2048,256]{1,0:T(8,128)} %b_ref.7, f32[4,2048,256]{2,1,0:T(8,128)} %u_ref.7), custom_call_target="tpu_custom_call" | custom-call | flops 4026531840 | bytes 13893632 | tf_op jit(solution)/shard_map/pallas_call | solution.py:70
  9.6 1.9 %collective-permute-done = f32[256,640]{1,0:T(8,128)S(1)} collective-permute-done((f32[256,640]{1,0:T(8,128)}, f32[256,640]{1,0:T(8,128)S(1)}, u32[]{:S(2)}, u32[]{:S(2)}) %collective-permute-start) | collective-permute-done | bytes 655392 | tf_op jit(solution)/shard_map/ppermute | solution.py:195
  12.7 2.9 %collective-permute-start.1 = (f32[256,640]{1,0:T(8,128)S(1)}, f32[256,640]{1,0:T(8,128)S(1)}, u32[]{:S(2)}, u32[]{:S(2)}) collective-permute-start(f32[256,640]{1,0:T(8,128)S(1)} %add.37.own_ref), channel_id=1, source_target_pairs={{0,2},{1,3},{2,0},{3,1},{4,6},{5,7},{6,4},{7,5},{8,10},{9,11},{10,... | collective-permute-start | bytes 1966088 | tf_op jit(solution)/shard_map/ppermute | solution.py:195
  15.6 9.1 %shard_map.38 = (f32[256,640]{1,0:T(8,128)}, f32[256,640]{1,0:T(8,128)}) custom-call(s32[1]{0:T(128)} %bitcast.par_ref, f32[4,2048,256]{2,1,0:T(8,128)} %v_ref.5, f32[2048,256]{1,0:T(8,128)} %b_ref.7, f32[4,2048,256]{2,1,0:T(8,128)} %u_ref.7), custom_call_target="tpu_custom_call" | custom-call | flops 4026531840 | bytes 13893632 | tf_op jit(solution)/shard_map/pallas_call | solution.py:70
  24.7 5.9 %collective-permute-done.1.sib_ref = f32[256,640]{1,0:T(8,128)S(1)} collective-permute-done((f32[256,640]{1,0:T(8,128)S(1)}, f32[256,640]{1,0:T(8,128)S(1)}, u32[]{:S(2)}, u32[]{:S(2)}) %collective-permute-start.1) | collective-permute-done | bytes 655392 | tf_op jit(solution)/shard_map/ppermute | solution.py:195
  31.3 1.6 collective-permute-done.4
  36.6 6.0 %shard_map.39 = (f32[256,512]{1,0:T(8,128)}, f32[168,512]{1,0:T(8,128)}, f32[88,512]{1,0:T(8,128)}) custom-call(s32[1]{0:T(128)} %bitcast.par_ref, f32[256,640]{1,0:T(8,128)} %copy-done.3, f32[256,640]{1,0:T(8,128)} %copy-done.16, f32[256,128]{1,0:T(8,128)} %copy-done.21, f32[256,128]{1,0:T(8,128)} %copy-done.23, f32[256,512]{1,0:T(8,128)} %slice.107.row_ref, ...), custom_call_target="tpu_custom_call" | custom-call | flops 3000000000 | bytes 4000000 | tf_op jit(solution)/shard_map/pallas_call | solution.py:145
  42.6 1.7 %collective-permute-start.6 = (f32[168,512]{1,0:T(8,128)}, f32[168,512]{1,0:T(8,128)S(1)}, u32[]{:S(2)}, u32[]{:S(2)}) collective-permute-start(f32[168,512]{1,0:T(8,128)} %get-tuple-element.38), channel_id=1, source_target_pairs={{0,2},{1,3},{2,0},{3,1},{4,6},{5,7},{6,4},{7,5},{8,10},{9,11},{10,... | collective-permute-start | bytes 1032200 | tf_op jit(solution)/shard_map/ppermute | solution.py:195
  45.9 13.1 %shard_map.40 = (f32[512,640]{1,0:T(8,128)}, f32[512,640]{1,0:T(8,128)}) custom-call(s32[1]{0:T(128)} %bitcast.par_ref, f32[4,2048,256]{2,1,0:T(8,128)} %v_ref.5, f32[2048,256]{1,0:T(8,128)} %b_ref.7, f32[4,2048,256]{2,1,0:T(8,128)} %u_ref.7), custom_call_target="tpu_custom_call" | custom-call | flops 8053063680 | bytes 17301504 | tf_op jit(solution)/shard_map/pallas_call | solution.py:70
  60.7 1.6 collective-permute-done.12
  62.7 8.3 %collective-permute-done.8 = f32[176,512]{1,0:T(8,128)} collective-permute-done((f32[176,512]{1,0:T(8,128)}, f32[176,512]{1,0:T(8,128)}, u32[]{:S(2)}, u32[]{:S(2)}) %collective-permute-start.8) | collective-permute-done | bytes 360480 | tf_op jit(solution)/shard_map/ppermute | solution.py:195
  77.4 5.5 %shard_map.41 = (f32[256,384]{1,0:T(8,128)}, f32[256,384]{1,0:T(8,128)}) custom-call(s32[1]{0:T(128)} %bitcast.par_ref, f32[256,512]{1,0:T(8,128)} %pad_maximum_fusion.own_ref, f32[256,512]{1,0:T(8,128)} %pad_maximum_fusion.1.sib_ref, f32[256,128]{1,0:T(8,128)} %copy-done.25, f32[256,128]{1,0:T(8,128)} %copy-done.19, f32[256,384]{1,0:T(8,128)} %slice.117.row_ref, ...), custom_call_target="tpu_custom_call" | custom-call | flops 3000000000 | bytes 4000000 | tf_op jit(solution)/shard_map/pallas_call | solution.py:145
  83.5 7.5 %collective-permute-done.15 = f32[256,384]{1,0:T(8,128)S(1)} collective-permute-done((f32[256,384]{1,0:T(8,128)}, f32[256,384]{1,0:T(8,128)S(1)}, u32[]{:S(2)}, u32[]{:S(2)}) %collective-permute-start.15) | collective-permute-done | bytes 393248 | tf_op jit(solution)/shard_map/ppermute | solution.py:195
  92.6 7.3 %collective-permute-done.16 = f32[256,384]{1,0:T(8,128)S(1)} collective-permute-done((f32[256,384]{1,0:T(8,128)S(1)}, f32[256,384]{1,0:T(8,128)S(1)}, u32[]{:S(2)}, u32[]{:S(2)}) %collective-permute-start.16) | collective-permute-done | bytes 393248 | tf_op jit(solution)/shard_map/ppermute | solution.py:195
  102.0 7.7 %collective-permute-done.17.sib_ref = f32[256,384]{1,0:T(8,128)S(1)} collective-permute-done((f32[256,384]{1,0:T(8,128)S(1)}, f32[256,384]{1,0:T(8,128)S(1)}, u32[]{:S(2)}, u32[]{:S(2)}) %collective-permute-start.17) | collective-permute-done | bytes 393248 | tf_op jit(solution)/shard_map/ppermute | solution.py:195
  112.0 4.4 %shard_map.42 = (f32[256,256]{1,0:T(8,128)}, f32[256,256]{1,0:T(8,128)}) custom-call(s32[1]{0:T(128)} %bitcast.par_ref, f32[256,384]{1,0:T(8,128)} %copy-done.7, f32[256,384]{1,0:T(8,128)} %copy-done.15, f32[256,128]{1,0:T(8,128)} %copy-done.27, f32[256,128]{1,0:T(8,128)} %copy-done.29, f32[256,256]{1,0:T(8,128)} %slice.125.row_ref, f32[256,128]{1,0:T(8,128)} %copy-done.11, ...), custom_call_target="tpu_custom_call" | custom-call | flops 3000000000 | bytes 4000000 | tf_op jit(solution)/shard_map/pallas_call | solution.py:145
  116.9 6.0 %collective-permute-done.21 = f32[256,256]{1,0:T(8,128)S(1)} collective-permute-done((f32[256,256]{1,0:T(8,128)}, f32[256,256]{1,0:T(8,128)S(1)}, u32[]{:S(2)}, u32[]{:S(2)}) %collective-permute-start.21) | collective-permute-done | bytes 262176 | tf_op jit(solution)/shard_map/ppermute | solution.py:195
  124.5 5.9 %collective-permute-done.22 = f32[256,256]{1,0:T(8,128)S(1)} collective-permute-done((f32[256,256]{1,0:T(8,128)S(1)}, f32[256,256]{1,0:T(8,128)S(1)}, u32[]{:S(2)}, u32[]{:S(2)}) %collective-permute-start.22) | collective-permute-done | bytes 262176 | tf_op jit(solution)/shard_map/ppermute | solution.py:195
  131.6 5.3 %collective-permute-done.23 = f32[256,256]{1,0:T(8,128)S(1)} collective-permute-done((f32[256,256]{1,0:T(8,128)S(1)}, f32[256,256]{1,0:T(8,128)S(1)}, u32[]{:S(2)}, u32[]{:S(2)}) %collective-permute-start.23) | collective-permute-done | bytes 262176 | tf_op jit(solution)/shard_map/ppermute | solution.py:195
  136.9 2.7 %collective-permute-start.24 = (f32[256,256]{1,0:T(8,128)S(1)}, f32[256,256]{1,0:T(8,128)S(1)}, u32[]{:S(2)}, u32[]{:S(2)}) collective-permute-start(f32[256,256]{1,0:T(8,128)S(1)} %add.47.own_ref), channel_id=1, source_target_pairs={{0,16},{1,17},{2,18},{3,19},{4,20},{5,21},{6,22},{7,23},{8,24},{9,... | collective-permute-start | bytes 786440 | tf_op jit(solution)/shard_map/ppermute | solution.py:195
  140.4 9.2 %collective-permute-done.24.sib_ref = f32[256,256]{1,0:T(8,128)S(1)} collective-permute-done((f32[256,256]{1,0:T(8,128)S(1)}, f32[256,256]{1,0:T(8,128)S(1)}, u32[]{:S(2)}, u32[]{:S(2)}) %collective-permute-start.24) | collective-permute-done | bytes 262176 | tf_op jit(solution)/shard_map/ppermute | solution.py:195
  151.7 5.3 %shard_map.43.w_ref = f32[1024,128]{1,0:T(8,128)} custom-call(s32[1]{0:T(128)} %bitcast.par_ref, f32[256,256]{1,0:T(8,128)} %copy-done.8, f32[256,256]{1,0:T(8,128)} %copy-done.14, f32[256,128]{1,0:T(8,128)} %copy-done.22, f32[256,128]{1,0:T(8,128)} %copy-done.26, f32[256,256]{1,0:T(8,128)} %get-tuple-element.50.refs_0_, ...), custom_call_target="tpu_custom_call" | custom-call | flops 3000000000 | bytes 4000000 | tf_op jit(solution)/shard_map/pallas_call | solution.py:145
  157.2 2.0 %collective-permute-done.30.w_other_ref = f32[1024,128]{1,0:T(8,128)S(1)} collective-permute-done((f32[1024,128]{1,0:T(8,128)}, f32[1024,128]{1,0:T(8,128)S(1)}, u32[]{:S(2)}, u32[]{:S(2)}) %collective-permute-start.30) | collective-permute-done | bytes 524320 | tf_op jit(solution)/shard_map/ppermute | solution.py:195
  159.9 8.1 %shard_map.44 = f32[2048,256]{1,0:T(8,128)} custom-call(s32[1]{0:T(128)} %bitcast.par_ref, f32[2048,256]{1,0:T(8,128)} %b_ref.7, f32[4,2048,256]{2,1,0:T(8,128)} %u_ref.7, f32[1024,128]{1,0:T(8,128)} %shard_map.43.w_ref, f32[1024,128]{1,0:T(8,128)} %copy-done.9), custom_call_target="tpu_custom_call" | custom-call | tf_op jit(solution)/shard_map/pallas_call | solution.py:175
  (141 shorter events, 29.3 us)
Async XLA Ops:
  12.7 18.0 %collective-permute-start.1 = (f32[256,640]{1,0:T(8,128)S(1)}, f32[256,640]{1,0:T(8,128)S(1)}, u32[]{:S(2)}, u32[]{:S(2)}) collective-permute-start(f32[256,640]{1,0:T(8,128)S(1)} %add.37.own_ref), channel_id=1, source_target_pairs={{0,2},{1,3},{2,0},{3,1},{4,6},{5,7},{6,4},{7,5},{8,10},{9,11},{10,... | collective-permute-start | bytes 1966088 | tf_op jit(solution)/shard_map/ppermute | solution.py:195
  30.7 4.6 %collective-permute-start.2 = (f32[256,128]{1,0:T(8,128)S(1)}, f32[256,128]{1,0:T(8,128)S(1)}, u32[]{:S(2)}, u32[]{:S(2)}) collective-permute-start(f32[256,128]{1,0:T(8,128)S(1)} %slice.82), channel_id=1, source_target_pairs={{0,1},{1,0},{2,3},{3,2},{4,5},{5,4},{6,7},{7,6},{8,9},{9,8},{10,11... | collective-permute-start | bytes 393224 | tf_op jit(solution)/shard_map/ppermute | solution.py:195
  31.2 4.0 %collective-permute-start.3 = (f32[256,128]{1,0:T(8,128)S(1)}, f32[256,128]{1,0:T(8,128)S(1)}, u32[]{:S(2)}, u32[]{:S(2)}) collective-permute-start(f32[256,128]{1,0:T(8,128)S(1)} %slice.83), channel_id=1, source_target_pairs={{0,1},{1,0},{2,3},{3,2},{4,5},{5,4},{6,7},{7,6},{8,9},{9,8},{10,11... | collective-permute-start | bytes 393224 | tf_op jit(solution)/shard_map/ppermute | solution.py:195
  42.6 16.4 %collective-permute-start.6 = (f32[168,512]{1,0:T(8,128)}, f32[168,512]{1,0:T(8,128)S(1)}, u32[]{:S(2)}, u32[]{:S(2)}) collective-permute-start(f32[168,512]{1,0:T(8,128)} %get-tuple-element.38), channel_id=1, source_target_pairs={{0,2},{1,3},{2,0},{3,1},{4,6},{5,7},{6,4},{7,5},{8,10},{9,11},{10,... | collective-permute-start | bytes 1032200 | tf_op jit(solution)/shard_map/ppermute | solution.py:195
  44.3 14.7 %collective-permute-start.7 = (f32[88,512]{1,0:T(8,128)}, f32[88,512]{1,0:T(8,128)S(1)}, u32[]{:S(2)}, u32[]{:S(2)}) collective-permute-start(f32[88,512]{1,0:T(8,128)} %get-tuple-element.39), channel_id=1, source_target_pairs={{0,4},{1,5},{2,6},{3,7},{4,0},{5,1},{6,2},{7,3},{8,12},{9,13},{10,... | collective-permute-start | bytes 540680 | tf_op jit(solution)/shard_map/ppermute | solution.py:195
  59.0 3.3 %collective-permute-start.12 = (f32[512,640]{1,0:T(8,128)}, f32[512,640]{1,0:T(8,128)S(1)}, u32[]{:S(2)}, u32[]{:S(2)}) collective-permute-start(f32[512,640]{1,0:T(8,128)} %get-tuple-element.45), channel_id=1, source_target_pairs={{0,1},{1,0},{2,3},{3,2},{4,5},{5,4},{6,7},{7,6},{8,9},{9,8},{10,11... | collective-permute-start | bytes 3932168 | tf_op jit(solution)/shard_map/ppermute | solution.py:195
  59.8 11.1 %collective-permute-start.8 = (f32[176,512]{1,0:T(8,128)}, f32[176,512]{1,0:T(8,128)}, u32[]{:S(2)}, u32[]{:S(2)}) collective-permute-start(f32[176,512]{1,0:T(8,128)} %pad_maximum_fusion.2), channel_id=1, source_target_pairs={{0,2},{1,3},{2,0},{3,1},{4,6},{5,7},{6,4},{7,5},{8,10},{9,11},{10,... | collective-permute-start | bytes 1081352 | tf_op jit(solution)/shard_map/ppermute | solution.py:195
  60.4 11.6 %collective-permute-start.9 = (f32[168,512]{1,0:T(8,128)S(1)}, f32[168,512]{1,0:T(8,128)S(1)}, u32[]{:S(2)}, u32[]{:S(2)}) collective-permute-start(f32[168,512]{1,0:T(8,128)S(1)} %add.39), channel_id=1, source_target_pairs={{0,4},{1,5},{2,6},{3,7},{4,0},{5,1},{6,2},{7,3},{8,12},{9,13},{10,... | collective-permute-start | bytes 1032200 | tf_op jit(solution)/shard_map/ppermute | solution.py:195
  62.5 9.7 %collective-permute-start.13 = (f32[512,128]{1,0:T(8,128)S(1)}, f32[512,128]{1,0:T(8,128)S(1)}, u32[]{:S(2)}, u32[]{:S(2)}) collective-permute-start(f32[512,128]{1,0:T(8,128)S(1)} %slice.116), channel_id=1, source_target_pairs={{0,1},{1,0},{2,3},{3,2},{4,5},{5,4},{6,7},{7,6},{8,9},{9,8},{10,11... | collective-permute-start | bytes 786440 | tf_op jit(solution)/shard_map/ppermute | solution.py:195
  72.1 4.7 %collective-permute-start.11 = (f32[256,128]{1,0:T(8,128)S(1)}, f32[256,128]{1,0:T(8,128)S(1)}, u32[]{:S(2)}, u32[]{:S(2)}) collective-permute-start(f32[256,128]{1,0:T(8,128)S(1)} %fusion.12), channel_id=1, source_target_pairs={{0,1},{1,0},{2,3},{3,2},{4,5},{5,4},{6,7},{7,6},{8,9},{9,8},{10,11... | collective-permute-start | bytes 393224 | tf_op jit(solution)/shard_map/ppermute | solution.py:195
  73.4 3.3 %collective-permute-start.10 = (f32[256,128]{1,0:T(8,128)S(1)}, f32[256,128]{1,0:T(8,128)S(1)}, u32[]{:S(2)}, u32[]{:S(2)}) collective-permute-start(f32[256,128]{1,0:T(8,128)S(1)} %fusion.13), channel_id=1, source_target_pairs={{0,1},{1,0},{2,3},{3,2},{4,5},{5,4},{6,7},{7,6},{8,9},{9,8},{10,11... | collective-permute-start | bytes 393224 | tf_op jit(solution)/shard_map/ppermute | solution.py:195
  83.0 8.0 %collective-permute-start.15 = (f32[256,384]{1,0:T(8,128)}, f32[256,384]{1,0:T(8,128)S(1)}, u32[]{:S(2)}, u32[]{:S(2)}) collective-permute-start(f32[256,384]{1,0:T(8,128)} %get-tuple-element.47), channel_id=1, source_target_pairs={{0,2},{1,5},{2,0},{3,7},{4,6},{5,1},{6,4},{7,3},{8,10},{9,13},{10,... | collective-permute-start | bytes 1179656 | tf_op jit(solution)/shard_map/ppermute | solution.py:195
  92.0 7.8 %collective-permute-start.16 = (f32[256,384]{1,0:T(8,128)S(1)}, f32[256,384]{1,0:T(8,128)S(1)}, u32[]{:S(2)}, u32[]{:S(2)}) collective-permute-start(f32[256,384]{1,0:T(8,128)S(1)} %add.43), channel_id=1, source_target_pairs={{0,4},{1,3},{2,6},{3,1},{4,0},{5,7},{6,2},{7,5},{8,12},{9,11},{10,... | collective-permute-start | bytes 1179656 | tf_op jit(solution)/shard_map/ppermute | solution.py:195
  99.9 9.9 %collective-permute-start.17 = (f32[256,384]{1,0:T(8,128)S(1)}, f32[256,384]{1,0:T(8,128)S(1)}, u32[]{:S(2)}, u32[]{:S(2)}) collective-permute-start(f32[256,384]{1,0:T(8,128)S(1)} %add.44.own_ref), channel_id=1, source_target_pairs={{0,8},{1,9},{2,10},{3,11},{4,12},{5,13},{6,14},{7,15},{8,0},{9,1},... | collective-permute-start | bytes 1179656 | tf_op jit(solution)/shard_map/ppermute | solution.py:195
  101.4 9.2 %collective-permute-start.20 = (f32[256,128]{1,0:T(8,128)S(1)}, f32[256,128]{1,0:T(8,128)S(1)}, u32[]{:S(2)}, u32[]{:S(2)}) collective-permute-start(f32[256,128]{1,0:T(8,128)S(1)} %slice.126.col_ref), channel_id=1, source_target_pairs={{0,1},{1,0},{2,3},{3,2},{4,5},{5,4},{6,7},{7,6},{8,9},{9,8},{10,11... | collective-permute-start | bytes 393224 | tf_op jit(solution)/shard_map/ppermute | solution.py:195
  101.5 9.2 %collective-permute-start.18 = (f32[256,128]{1,0:T(8,128)S(1)}, f32[256,128]{1,0:T(8,128)S(1)}, u32[]{:S(2)}, u32[]{:S(2)}) collective-permute-start(f32[256,128]{1,0:T(8,128)S(1)} %slice.120), channel_id=1, source_target_pairs={{0,1},{1,0},{2,3},{3,2},{4,5},{5,4},{6,7},{7,6},{8,9},{9,8},{10,11... | collective-permute-start | bytes 393224 | tf_op jit(solution)/shard_map/ppermute | solution.py:195
  116.4 6.6 %collective-permute-start.21 = (f32[256,256]{1,0:T(8,128)}, f32[256,256]{1,0:T(8,128)S(1)}, u32[]{:S(2)}, u32[]{:S(2)}) collective-permute-start(f32[256,256]{1,0:T(8,128)} %get-tuple-element.49), channel_id=1, source_target_pairs={{0,2},{1,5},{2,0},{3,7},{4,6},{5,1},{6,4},{7,3},{8,10},{9,13},{10,... | collective-permute-start | bytes 786440 | tf_op jit(solution)/shard_map/ppermute | solution.py:195
  124.0 6.4 %collective-permute-start.22 = (f32[256,256]{1,0:T(8,128)S(1)}, f32[256,256]{1,0:T(8,128)S(1)}, u32[]{:S(2)}, u32[]{:S(2)}) collective-permute-start(f32[256,256]{1,0:T(8,128)S(1)} %add.45), channel_id=1, source_target_pairs={{0,4},{1,9},{2,6},{3,11},{4,0},{5,13},{6,2},{7,15},{8,12},{9,1},{1... | collective-permute-start | bytes 786440 | tf_op jit(solution)/shard_map/ppermute | solution.py:195
  130.4 6.4 %collective-permute-start.23 = (f32[256,256]{1,0:T(8,128)S(1)}, f32[256,256]{1,0:T(8,128)S(1)}, u32[]{:S(2)}, u32[]{:S(2)}) collective-permute-start(f32[256,256]{1,0:T(8,128)S(1)} %add.46), channel_id=1, source_target_pairs={{0,8},{1,3},{2,10},{3,1},{4,12},{5,7},{6,14},{7,5},{8,0},{9,11},{1... | collective-permute-start | bytes 786440 | tf_op jit(solution)/shard_map/ppermute | solution.py:195
  131.5 18.1 %collective-permute-start.29 = (f32[256,384]{1,0:T(8,128)S(1)}, f32[256,384]{1,0:T(8,128)S(1)}, u32[]{:S(2)}, u32[]{:S(2)}) collective-permute-start(f32[256,384]{1,0:T(8,128)S(1)} %slice.106), channel_id=1, source_target_pairs={{0,1},{1,0},{2,3},{3,2},{4,5},{5,4},{6,7},{7,6},{8,9},{9,8},{10,11... | collective-permute-start | bytes 1179656 | tf_op jit(solution)/shard_map/ppermute | solution.py:195
  136.9 12.7 %collective-permute-start.24 = (f32[256,256]{1,0:T(8,128)S(1)}, f32[256,256]{1,0:T(8,128)S(1)}, u32[]{:S(2)}, u32[]{:S(2)}) collective-permute-start(f32[256,256]{1,0:T(8,128)S(1)} %add.47.own_ref), channel_id=1, source_target_pairs={{0,16},{1,17},{2,18},{3,19},{4,20},{5,21},{6,22},{7,23},{8,24},{9,... | collective-permute-start | bytes 786440 | tf_op jit(solution)/shard_map/ppermute | solution.py:195
  139.6 10.1 %collective-permute-start.28 = (f32[256,256]{1,0:T(8,128)S(1)}, f32[256,256]{1,0:T(8,128)S(1)}, u32[]{:S(2)}, u32[]{:S(2)}) collective-permute-start(f32[256,256]{1,0:T(8,128)S(1)} %slice.105), channel_id=1, source_target_pairs={{0,1},{1,0},{2,3},{3,2},{4,5},{5,4},{6,7},{7,6},{8,9},{9,8},{10,11... | collective-permute-start | bytes 786440 | tf_op jit(solution)/shard_map/ppermute | solution.py:195
  139.7 10.0 %collective-permute-start.27 = (f32[256,128]{1,0:T(8,128)S(1)}, f32[256,128]{1,0:T(8,128)S(1)}, u32[]{:S(2)}, u32[]{:S(2)}) collective-permute-start(f32[256,128]{1,0:T(8,128)S(1)} %slice.104), channel_id=1, source_target_pairs={{0,1},{1,0},{2,3},{3,2},{4,5},{5,4},{6,7},{7,6},{8,9},{9,8},{10,11... | collective-permute-start | bytes 393224 | tf_op jit(solution)/shard_map/ppermute | solution.py:195
  140.3 9.5 %collective-permute-start.25 = (f32[256,128]{1,0:T(8,128)S(1)}, f32[256,128]{1,0:T(8,128)S(1)}, u32[]{:S(2)}, u32[]{:S(2)}) collective-permute-start(f32[256,128]{1,0:T(8,128)S(1)} %slice.127), channel_id=1, source_target_pairs={{0,1},{1,0},{2,3},{3,2},{4,5},{5,4},{6,7},{7,6},{8,9},{9,8},{10,11... | collective-permute-start | bytes 393224 | tf_op jit(solution)/shard_map/ppermute | solution.py:195
  (37 other events, 177.8 us)
